TPU v7x, 256 devices: a whole 4x4x8 slice. The times are simulated.
256 devices in a mesh: ctx: 8 (over z), row: 2 (over core), exp: 16 (over x, y).
Axes of the slice: x: 4, y: 4, z: 8, core: 2. Of those that a mesh axis runs over, the one named last changes fastest.
Arguments:
- queries: bfloat16 [128, 128, 576], P(('row', 'exp')), may hold values from -10 to 10
- latent_cache: bfloat16 [128, 8192, 576], P(('row', 'exp'), 'ctx'), may hold values from -6 to 6
- lengths: int32 [128], P(('row', 'exp')), may hold values from 512 to 8192, as said below
- w_value: bfloat16 [128, 512, 128], P(('ctx', 'exp')), may hold values from -0.25 to 0.25
- w_out: bfloat16 [16384, 7168], P(('ctx', 'exp')), may hold values from -0.1875 to 0.1875
- stream: bfloat16 [128, 7168], P(('row', 'exp'), 'ctx'), may hold values from -6 to 6
- norm_gain: float32 [7168], P('ctx'), may hold values from 0.1 to 1.9
- expert_ids: int32 [128, 8], P(('row', 'exp')), may hold values from 0 to 31, all different within a row; in each aligned block of 4 rows (0 to 3, 4 to 7, ...) at most 2 rows name the same one
- gate_weights: float32 [128, 8], P(('row', 'exp')), may hold values from 0.1 to 0.6
- w_gate: bfloat16 [32, 7168, 1024], P(('row', 'exp'), 'ctx'), may hold values from -0.0625 to 0.0625
- w_up: bfloat16 [32, 7168, 1024], P(('row', 'exp'), 'ctx'), may hold values from -0.0625 to 0.0625
- w_down: bfloat16 [32, 1024, 7168], P(('row', 'exp'), None, 'ctx'), may hold values from -0.1875 to 0.1875
Outputs:
- layer_out: bfloat16 [128, 7168], P(('row', 'exp'), 'ctx')
Inputs may be any that keep to these rules, and one draw needn't show every extreme that they name: `lengths`: some row has 8192 live positions and some row 512. `expert_ids`: each row names 8 different experts; among the 4 rows of one device no expert is named by more than 2 rows.
All inputs are finite; a program needn't handle non-finite values.
Results may differ from a plain program's by a relative error of at most 0.012.
Values may be sent and summed in bfloat16 or wider, within the bound.
No kernel may reach another device: no remote copies, remote signals or barrier semaphores. Data moves between devices by JAX's collectives and lax.ppermute only.
A program may use at most 64 MiB of HBM per device.

v0:
```python
import jax
import jax.numpy as jnp
from jax import lax
from jax.sharding import PartitionSpec as P

D = 7168
QK_HEAD = 192


epsilon = 1e-06


def merge_blocks(outputs, maxima, totals):
    top_value = jnp.max(maxima, axis=0)
    factor = jnp.exp(maxima - top_value[None])
    numer = jnp.sum(factor[..., None] * outputs, axis=0)
    denom = jnp.sum(factor * totals, axis=0)
    return (numer / denom[..., None]).astype(jnp.bfloat16)


def on_device(
    queries,
    latent_cache,
    lengths,
    w_value,
    w_out,
    stream,
    norm_gain,
    expert_ids,
    gate_weights,
    w_gate,
    w_up,
    w_down,
):
    n_ctx = lax.axis_size("ctx")
    n_row = lax.axis_size("row")
    n_exp = lax.axis_size("exp")
    groups = queries.shape[0]
    block = latent_cache.shape[1]
    per_dev = w_value.shape[0]
    latent = w_value.shape[1]
    scores = jnp.einsum(
        "bhw,btw->bht", queries, latent_cache, preferred_element_type=jnp.float32
    ) * QK_HEAD ** (-0.5)
    position = lax.axis_index("ctx") * block + jnp.arange(block, dtype=jnp.int32)
    live = (position[None, :] < lengths[:, None])[:, None, :]
    block_max = jnp.max(jnp.where(live, scores, -jnp.inf), axis=2)
    shift_by = jnp.where(jnp.isfinite(block_max), block_max, 0.0)
    weights = jnp.where(live, jnp.exp(scores - shift_by[..., None]), 0.0)
    totals = jnp.sum(weights, axis=2)
    latent_out = jnp.einsum(
        "bht,btl->bhl",
        weights.astype(jnp.bfloat16),
        latent_cache[:, :, :latent],
        preferred_element_type=jnp.float32,
    )
    outputs, maxima, sums = (
        lax.all_to_all(
            latent_out.reshape(1, groups, n_ctx * n_exp, per_dev, latent),
            ("ctx", "exp"),
            split_axis=2,
            concat_axis=0,
            tiled=True,
        ),
        lax.all_to_all(
            block_max.reshape(1, groups, n_ctx * n_exp, per_dev),
            ("ctx", "exp"),
            split_axis=2,
            concat_axis=0,
            tiled=True,
        ),
        lax.all_to_all(
            totals.reshape(1, groups, n_ctx * n_exp, per_dev),
            ("ctx", "exp"),
            split_axis=2,
            concat_axis=0,
            tiled=True,
        ),
    )
    gathered_rows = n_exp * groups
    attended = merge_blocks(
        outputs.reshape(n_ctx, gathered_rows, per_dev, latent),
        maxima.reshape(n_ctx, gathered_rows, per_dev),
        sums.reshape(n_ctx, gathered_rows, per_dev),
    )
    values = jnp.einsum("nhl,hlv->nhv", attended, w_value, preferred_element_type=jnp.float32)
    values = values.astype(jnp.bfloat16).reshape(gathered_rows, -1)
    split_out = w_out.reshape(w_out.shape[0], n_ctx, -1)
    term_rows = jnp.einsum(
        "nk,kcd->cnd", values, split_out, preferred_element_type=jnp.float32
    ).reshape(n_ctx * gathered_rows, -1)
    attn_out = lax.psum_scatter(term_rows, ("ctx", "exp"), scatter_dimension=0, tiled=True)
    hidden = lax.optimization_barrier((stream.astype(jnp.float32) + attn_out).astype(jnp.bfloat16))
    experts = n_row * n_exp
    picks = expert_ids.shape[1]
    capacity = max(2, (groups * picks + experts - 1) // experts)
    expert_range = jnp.arange(experts, dtype=jnp.int32)
    onehot = expert_ids[:, :, None] == expert_range[None, None, :]
    named = jnp.sum(onehot.astype(jnp.int32), axis=1)
    slot_of = jnp.cumsum(named, axis=0) - named
    slot_match = slot_of[:, :, None] == jnp.arange(capacity, dtype=jnp.int32)[None, None, :]
    placed = (named[:, :, None] == 1) & slot_match
    outgoing = jnp.einsum(
        "bxs,bd->xsd", placed.astype(jnp.bfloat16), hidden, preferred_element_type=jnp.float32
    ).astype(jnp.bfloat16)
    width_dev = outgoing.shape[2]
    arrived = lax.all_to_all(outgoing, ("row", "exp"), split_axis=0, concat_axis=0, tiled=True)
    arrived = arrived.reshape(experts * capacity, width_dev)
    arrived_wide = arrived.astype(jnp.float32)
    sumsq = jnp.sum(arrived_wide * arrived_wide, axis=1)
    scaled = (arrived_wide * norm_gain[None, :]).astype(jnp.bfloat16)
    gate_part = jnp.dot(scaled, w_gate[0], preferred_element_type=jnp.float32)
    up_part = jnp.dot(scaled, w_up[0], preferred_element_type=jnp.float32)
    gate_part, up_part, sumsq = lax.psum((gate_part, up_part, sumsq), "ctx")
    inverse = lax.rsqrt(sumsq / D + epsilon)[:, None]
    active = (jax.nn.silu(inverse * gate_part) * (inverse * up_part)).astype(jnp.bfloat16)
    produced = jnp.dot(active, w_down[0], preferred_element_type=jnp.float32).astype(jnp.bfloat16)
    returned = lax.all_to_all(
        produced.reshape(experts, capacity, width_dev),
        ("row", "exp"),
        split_axis=0,
        concat_axis=0,
        tiled=True,
    )
    weighted = jnp.sum(gate_weights[:, :, None] * onehot.astype(jnp.float32), axis=1)
    combine = weighted[:, :, None] * slot_match.astype(jnp.float32)
    mixture = jnp.einsum(
        "bxs,xsd->bd", combine, returned.astype(jnp.float32), precision=lax.Precision.HIGHEST
    )
    return (hidden.astype(jnp.float32) + mixture).astype(jnp.bfloat16)


def solution(mesh):
    placed = (
        P(("row", "exp"), None, None),
        P(("row", "exp"), "ctx", None),
        P(("row", "exp")),
        P(("ctx", "exp"), None, None),
        P(("ctx", "exp"), None),
        P(("row", "exp"), "ctx"),
        P("ctx"),
        P(("row", "exp"), None),
        P(("row", "exp"), None),
        P(("row", "exp"), "ctx", None),
        P(("row", "exp"), "ctx", None),
        P(("row", "exp"), None, "ctx"),
    )
    return jax.shard_map(
        on_device, mesh=mesh, in_specs=placed, out_specs=P(("row", "exp"), "ctx"), check_vma=False
    )
```

profile of v0, /device:TPU:1, one launch (start us, length us, event | category | flops | bytes accessed | tf_op | source)
XLA Modules:
  0.0 436.3 jit_solution(4011889759420113957)
XLA Ops:
  6.5 0.9 broadcast_compare_fusion
  7.4 3.8 select_reduce_fusion
  11.3 1.3 copy-done.1
  13.9 16.3 %all-to-all-start.2 = ((f32[1,4,128,1]{1,3,0,2:T(1,128)}), f32[1,4,128,1]{1,3,0,2:T(1,128)S(1)}, u32[]{:S(2)}, u32[]{:S(2)}) async-start(f32[1,4,128,1]{1,3,0,2:T(1,128)} %copy.43), calls=%async_computation.2 | async-start | bytes 131072 | tf_op jit(solution)/shard_map/all_to_all | solution.py:72
  31.0 10.0 %all-to-all-done.2 = f32[1,4,128,1]{1,3,0,2:T(1,128)S(1)} async-done(((f32[1,4,128,1]{1,3,0,2:T(1,128)}), f32[1,4,128,1]{1,3,0,2:T(1,128)S(1)}, u32[]{:S(2)}, u32[]{:S(2)}) %all-to-all-start.2) | async-done | bytes 2080 | tf_op jit(solution)/shard_map/all_to_all | solution.py:72
  41.0 6.1 %all-to-all-start = ((f32[1,4,128,1]{1,3,0,2:T(1,128)}), f32[1,4,128,1]{1,3,0,2:T(1,128)S(1)}, u32[]{:S(2)}, u32[]{:S(2)}) async-start(f32[1,4,128,1]{1,3,0,2:T(1,128)} %copy.40), calls=%async_computation | async-start | bytes 131072 | tf_op jit(solution)/shard_map/all_to_all | solution.py:65
  47.1 4.4 fusion.13
  51.5 1.7 copy.42
  53.1 4.7 %all-to-all-done = f32[1,4,128,1]{1,3,0,2:T(1,128)S(1)} async-done(((f32[1,4,128,1]{1,3,0,2:T(1,128)}), f32[1,4,128,1]{1,3,0,2:T(1,128)S(1)}, u32[]{:S(2)}, u32[]{:S(2)}) %all-to-all-start) | async-done | bytes 2080 | tf_op jit(solution)/shard_map/all_to_all | solution.py:65
  57.8 8.5 %all-to-all-start.1 = ((f32[1,4,128,1,512]{4,1,3,0,2:T(4,128)}), f32[1,4,128,1,512]{4,1,3,0,2:T(4,128)S(1)}, u32[]{:S(2)}, u32[]{:S(2)}) async-start(f32[1,4,128,1,512]{4,1,3,0,2:T(4,128)} %copy.42), calls=%async_computation.1 | async-start | bytes 2097152 | tf_op jit(solution)/shard_map/all_to_all | solution.py:58
  66.9 26.3 %all-to-all-done.1 = f32[1,4,128,1,512]{4,1,3,0,2:T(4,128)S(1)} async-done(((f32[1,4,128,1,512]{4,1,3,0,2:T(4,128)}), f32[1,4,128,1,512]{4,1,3,0,2:T(4,128)S(1)}, u32[]{:S(2)}, u32[]{:S(2)}) %all-to-all-start.1) | async-done | bytes 1048608 | tf_op jit(solution)/shard_map/all_to_all | solution.py:58
  93.2 2.4 reshape.239
  95.6 2.3 multiply_reduce_fusion
  98.0 3.3 fusion.2
  102.8 217.9 %all-reduce.5.cloned.1.call-done = f32[512,896]{1,0:T(8,128)} async-done(((f32[512,896]{1,0:T(8,128)}), f32[512,896]{1,0:T(8,128)}) %all-reduce.5.cloned.1.call-update) | async-done | bytes 1835024
  321.7 16.9 %all_to_all.55 = bf16[32,2,896]{2,1,0:T(2,128)(2,1)S(1)} all-to-all(bf16[32,2,896]{2,1,0:T(2,128)(2,1)S(1)} %copy.45), channel_id=1, replica_groups=mesh['ctx'=8,'row'=2,'exp'=16] {'row','exp'}, dimensions={0} | all-to-all | bytes 229376 | tf_op jit(solution)/shard_map/all_to_all | solution.py:107
  339.0 1.1 fusion.7
  340.5 1.2 fusion.9
  341.9 12.7 %psum.21 = f32[64]{0:T(128)S(1)} all-reduce(f32[64]{0:T(128)S(1)} %reduce_sum.65), channel_id=1, replica_groups=mesh['ctx'=8,'row'=2,'exp'=16] {'ctx'}, use_global_device_ids=true, to_apply=%region_10.11 | all-reduce | flops 64 | bytes 512 | tf_op jit(solution)/shard_map/psum | solution.py:114
  354.6 51.5 %all-reduce.7.cloned.1.call-done = (f32[64,1024]{1,0:T(8,128)}, f32[64,1024]{1,0:T(8,128)}) async-done(((f32[64,1024]{1,0:T(8,128)}, f32[64,1024]{1,0:T(8,128)}), (f32[64,1024]{1,0:T(8,128)}, f32[64,1024]{1,0:T(8,128)})) %all-reduce.7.cloned.1.call-update) | async-done | bytes 524304 | tf_op jit(solution)/shard_map/psum | solution.py:114
  406.2 2.1 fusion.16
  409.0 12.2 %all-to-all-start.4 = ((bf16[32,2,896]{2,1,0:T(2,128)(2,1)}), bf16[32,2,896]{2,1,0:T(2,128)(2,1)S(1)}, u32[]{:S(2)}, u32[]{:S(2)}) async-start(bf16[32,2,896]{2,1,0:T(2,128)(2,1)} %reshape.246), calls=%async_computation.4 | async-start | bytes 229376 | tf_op jit(solution)/shard_map/all_to_all | solution.py:118
  421.3 7.3 %all-to-all-done.4 = bf16[32,2,896]{2,1,0:T(2,128)(2,1)S(1)} async-done(((bf16[32,2,896]{2,1,0:T(2,128)(2,1)}), bf16[32,2,896]{2,1,0:T(2,128)(2,1)S(1)}, u32[]{:S(2)}, u32[]{:S(2)}) %all-to-all-start.4) | async-done | bytes 114720 | tf_op jit(solution)/shard_map/all_to_all | solution.py:118
  428.6 0.8 fusion.21
  (48 shorter events, 6.2 us)
Async XLA Ops:
  6.5 332.4 %copy-start = (bf16[1,896,1024]{2,1,0:T(8,128)(2,1)S(1)}, bf16[1,896,1024]{2,1,0:T(8,128)(2,1)}, u32[]{:S(2)}) copy-start(bf16[1,896,1024]{2,1,0:T(8,128)(2,1)} %param.22) | copy-start | bytes 5505028
  11.2 1.4 copy-start.1
  13.9 27.1 %all-to-all-start.2 = ((f32[1,4,128,1]{1,3,0,2:T(1,128)}), f32[1,4,128,1]{1,3,0,2:T(1,128)S(1)}, u32[]{:S(2)}, u32[]{:S(2)}) async-start(f32[1,4,128,1]{1,3,0,2:T(1,128)} %copy.43), calls=%async_computation.2 | async-start | bytes 131072 | tf_op jit(solution)/shard_map/all_to_all | solution.py:72
  41.0 16.8 %all-to-all-start = ((f32[1,4,128,1]{1,3,0,2:T(1,128)}), f32[1,4,128,1]{1,3,0,2:T(1,128)S(1)}, u32[]{:S(2)}, u32[]{:S(2)}) async-start(f32[1,4,128,1]{1,3,0,2:T(1,128)} %copy.40), calls=%async_computation | async-start | bytes 131072 | tf_op jit(solution)/shard_map/all_to_all | solution.py:65
  57.8 35.4 %all-to-all-start.1 = ((f32[1,4,128,1,512]{4,1,3,0,2:T(4,128)}), f32[1,4,128,1,512]{4,1,3,0,2:T(4,128)S(1)}, u32[]{:S(2)}, u32[]{:S(2)}) async-start(f32[1,4,128,1,512]{4,1,3,0,2:T(4,128)} %copy.42), calls=%async_computation.1 | async-start | bytes 2097152 | tf_op jit(solution)/shard_map/all_to_all | solution.py:58
  66.3 31.6 %copy-start.3 = (bf16[1,512,128]{2,1,0:T(8,128)(2,1)S(1)}, bf16[1,512,128]{2,1,0:T(8,128)(2,1)}, u32[]{:S(2)}) copy-start(bf16[1,512,128]{2,1,0:T(8,128)(2,1)} %param.15) | copy-start | bytes 393220
  66.3 254.3 %all-reduce.5.cloned.1.call-start = ((), (), s32[]{:S(2)}) async-start(), calls=%async_computation.5 | async-start | bytes 3670016
  97.9 3.5 copy-start.4
  97.9 3.6 copy-start.8
  97.9 222.7 %copy-start.5 = (bf16[4,896]{1,0:T(4,128)(2,1)S(1)}, bf16[4,896]{1,0:T(4,128)(2,1)}, u32[]{:S(2)}) copy-start(bf16[4,896]{1,0:T(4,128)(2,1)} %param.17) | copy-start | bytes 21508
  101.3 237.4 %copy-start.6 = (f32[896]{0:T(1024)S(1)}, f32[896]{0:T(1024)}, u32[]{:S(2)}) copy-start(f32[896]{0:T(1024)} %param.18) | copy-start | bytes 10756
  101.3 304.9 %all-reduce.7.cloned.1.call-start = ((), (), s32[]{:S(2)}) async-start(), calls=%async_computation.6 | async-start | bytes 1048576 | tf_op jit(solution)/shard_map/psum | solution.py:114
  338.9 1.6 copy-start.2
  341.7 79.5 %copy-start.7 = (f32[4,8]{1,0:T(4,128)S(1)}, f32[4,8]{1,0:T(4,128)}, u32[]{:S(2)}) copy-start(f32[4,8]{1,0:T(4,128)} %param.20) | copy-start | bytes 388
  409.0 19.6 %all-to-all-start.4 = ((bf16[32,2,896]{2,1,0:T(2,128)(2,1)}), bf16[32,2,896]{2,1,0:T(2,128)(2,1)S(1)}, u32[]{:S(2)}, u32[]{:S(2)}) async-start(bf16[32,2,896]{2,1,0:T(2,128)(2,1)} %reshape.246), calls=%async_computation.4 | async-start | bytes 229376 | tf_op jit(solution)/shard_map/all_to_all | solution.py:118
Sparse Core Ops, SparseCore 0:
  101.4 219.1 all-reduce.4
  341.9 64.2 all-reduce.6
where the time goes:
time: 437 us; the launch traced here: 436 us
  waiting for transfers between devices  318 us (73%)
  starting transfers between devices  43.4 us (10%)
  blocking collectives  29.6 us (7%)
  matrix products  17 us (4%)
  between operations  14.3 us (3%)
  local copies, waits for them, and re-layouts  9.33 us (2%)
  other arithmetic  4.92 us (1%)
    unnamed x3, waiting for transfers between devices  218 us
    psum x1, waiting for transfers between devices, on_device(): gate_part, up_part, sumsq = lax.psum((gate_part, up_part, sumsq), 'ctx')  51.5 us
    all_to_all x1, waiting for transfers between devices, on_device(): lax.all_to_all(latent_out.reshape(1, groups, n_ctx * n_exp, per_dev, late...  26.3 us
    all_to_all x1, blocking collectives, on_device(): lax.all_to_all(outgoing, ('row', 'exp'), split_axis=0, concat_axis=0, til...  16.9 us
    all_to_all x1, starting transfers between devices, on_device(): lax.all_to_all(totals.reshape(1, groups, n_ctx * n_exp, per_dev), ('ctx',...  16.3 us
    psum x1, blocking collectives, on_device(): gate_part, up_part, sumsq = lax.psum((gate_part, up_part, sumsq), 'ctx')  12.7 us
    all_to_all x1, starting transfers between devices, on_device(): lax.all_to_all(produced.reshape(experts, capacity, width_dev), ('row', 'e...  12.2 us
    all_to_all x1, waiting for transfers between devices, on_device(): lax.all_to_all(totals.reshape(1, groups, n_ctx * n_exp, per_dev), ('ctx',...  10 us
  transfers between devices with their start and end apart: 6, of which 6 were waited for; matrix products, arithmetic and copies ran while one was open for 2% of the time, Pallas kernels for 0%

commit v1 on v0

v1 whole, which is shorter than its diff:
```python
import jax
import jax.numpy as jnp
from jax import lax
from jax.sharding import PartitionSpec as P

D = 7168
QK_HEAD = 192
BF = jnp.bfloat16
F32 = jnp.float32


epsilon = 1e-06


def exchange(x, axes):
    return lax.all_to_all(x, axes, split_axis=0, concat_axis=0, tiled=True)


def pieces(x):
    hi = x.astype(BF)
    rest = x - hi.astype(F32)
    mid = rest.astype(BF)
    low = (rest - mid.astype(F32)).astype(BF)
    return jnp.stack([hi, mid, low], axis=-1)


def on_device(
    queries,
    latent_cache,
    lengths,
    w_value,
    w_out,
    stream,
    norm_gain,
    expert_ids,
    gate_weights,
    w_gate,
    w_up,
    w_down,
):
    n_ctx = lax.axis_size("ctx")
    n_row = lax.axis_size("row")
    n_exp = lax.axis_size("exp")
    groups = queries.shape[0]
    heads = queries.shape[1]
    block = latent_cache.shape[1]
    latent = w_value.shape[1]
    width = stream.shape[1]
    scores = jnp.einsum(
        "bhw,btw->bht", queries, latent_cache, preferred_element_type=F32
    ) * QK_HEAD ** (-0.5)
    position = lax.axis_index("ctx") * block + jnp.arange(block, dtype=jnp.int32)
    live = (position[None, :] < lengths[:, None])[:, None, :]
    block_max = jnp.max(jnp.where(live, scores, -1e30), axis=2)
    weights = jnp.where(live, jnp.exp(scores - block_max[..., None]), 0.0)
    totals = jnp.sum(weights, axis=2)
    latent_out = jnp.einsum(
        "bht,btl->bhl", weights.astype(BF), latent_cache[:, :, :latent], preferred_element_type=F32
    )
    safe = jnp.where(totals > 0, totals, 1.0)
    lse = pieces(block_max + jnp.log(safe))
    per_ctx = heads // n_ctx
    part = (latent_out / safe[..., None]).astype(BF)
    part = part.reshape(groups, n_ctx, per_ctx, latent).transpose(1, 0, 2, 3)
    lse = lse.reshape(groups, n_ctx, per_ctx, 3).transpose(1, 0, 2, 3)
    lse = jnp.pad(lse.reshape(n_ctx, -1), ((0, 0), (0, 8 * latent - groups * per_ctx * 3)))
    sent = jnp.concatenate(
        [part.reshape(n_ctx, groups * per_ctx, latent), lse.reshape(n_ctx, 8, latent)], axis=1
    )
    got = exchange(sent, "ctx")
    lse = got[:, groups * per_ctx :].reshape(n_ctx, -1)[:, : groups * per_ctx * 3]
    lse = jnp.sum(lse.reshape(n_ctx, groups * per_ctx, 3).astype(F32), axis=-1)
    factor = jnp.exp(lse - jnp.max(lse, axis=0, keepdims=True))
    factor = factor / jnp.sum(factor, axis=0, keepdims=True)
    attended = jnp.sum(factor[..., None] * got[:, : groups * per_ctx].astype(F32), axis=0).astype(BF)
    attended = attended.reshape(groups, n_exp, latent).transpose(1, 0, 2)
    attended = exchange(attended.reshape(n_exp, groups * latent // 128, 128), "exp")
    gathered_rows = n_exp * groups
    attended = attended.reshape(gathered_rows, latent)
    values = jnp.dot(attended, w_value[0], preferred_element_type=F32).astype(BF)
    terms = jnp.dot(values, w_out, preferred_element_type=F32).astype(BF)
    terms = exchange(terms.reshape(n_exp, groups, D), "exp")
    terms = jnp.sum(terms.astype(F32), axis=0).astype(BF)
    terms = exchange(terms.reshape(groups, n_ctx, width).transpose(1, 0, 2), "ctx")
    attn_out = jnp.sum(terms.astype(F32), axis=0)
    hidden = lax.optimization_barrier((stream.astype(F32) + attn_out).astype(BF))
    experts = n_row * n_exp
    picks = expert_ids.shape[1]
    capacity = max(2, (groups * picks + experts - 1) // experts)
    expert_range = jnp.arange(experts, dtype=jnp.int32)
    onehot = expert_ids[:, :, None] == expert_range[None, None, :]
    named = jnp.sum(onehot.astype(jnp.int32), axis=1)
    slot_of = jnp.cumsum(named, axis=0) - named
    slot_match = slot_of[:, :, None] == jnp.arange(capacity, dtype=jnp.int32)[None, None, :]
    placed = (named[:, :, None] == 1) & slot_match
    outgoing = jnp.einsum("bxs,bd->xsd", placed.astype(BF), hidden, preferred_element_type=F32).astype(BF)
    arrived = exchange(outgoing, ("row", "exp")).reshape(experts * capacity, width)
    arrived_wide = arrived.astype(F32)
    sumsq = jnp.sum(arrived_wide * arrived_wide, axis=1)
    scaled = (arrived_wide * norm_gain[None, :]).astype(BF)
    gate_part = jnp.dot(scaled, w_gate[0], preferred_element_type=F32).astype(BF)
    up_part = jnp.dot(scaled, w_up[0], preferred_element_type=F32).astype(BF)
    extra = jnp.pad(pieces(sumsq), ((0, 0), (0, 125)))
    parts = jnp.concatenate([gate_part, up_part, extra], axis=1)
    per_dev = experts * capacity // n_ctx
    parts = exchange(parts.reshape(n_ctx, per_dev, parts.shape[1]), "ctx")
    sums = jnp.sum(parts.astype(F32), axis=0)
    hidden_units = w_gate.shape[2]
    gate_sum, up_sum = sums[:, :hidden_units], sums[:, hidden_units : 2 * hidden_units]
    sumsq = jnp.sum(sums[:, 2 * hidden_units : 2 * hidden_units + 3], axis=1)
    inverse = lax.rsqrt(sumsq / D + epsilon)[:, None]
    active = (jax.nn.silu(inverse * gate_sum) * (inverse * up_sum)).astype(BF)
    active = exchange(jnp.broadcast_to(active[None], (n_ctx,) + active.shape), "ctx")
    active = active.reshape(experts * capacity, hidden_units)
    produced = jnp.dot(active, w_down[0], preferred_element_type=F32).astype(BF)
    returned = exchange(produced.reshape(experts, capacity, width), ("row", "exp"))
    weighted = jnp.sum(gate_weights[:, :, None] * onehot.astype(F32), axis=1)
    combine = weighted[:, :, None] * slot_match.astype(F32)
    mixture = jnp.einsum("bxs,xsd->bd", combine, returned.astype(F32), precision=lax.Precision.HIGHEST)
    return (hidden.astype(F32) + mixture).astype(BF)


def solution(mesh):
    placed = (
        P(("row", "exp"), None, None),
        P(("row", "exp"), "ctx", None),
        P(("row", "exp")),
        P(("ctx", "exp"), None, None),
        P(("ctx", "exp"), None),
        P(("row", "exp"), "ctx"),
        P("ctx"),
        P(("row", "exp"), None),
        P(("row", "exp"), None),
        P(("row", "exp"), "ctx", None),
        P(("row", "exp"), "ctx", None),
        P(("row", "exp"), None, "ctx"),
    )
    return jax.shard_map(
        on_device, mesh=mesh, in_specs=placed, out_specs=P(("row", "exp"), "ctx"), check_vma=False
    )
```

time: 437 us -> 147 us (0.34)
  waiting for transfers between devices: 318 us -> 25.6 us
  blocking collectives: 29.6 us -> 80 us
  starting transfers between devices: 43.4 us -> 14.8 us
  between operations: 14.3 us -> 0.34 us
  local copies, waits for them, and re-layouts: 9.33 us -> 4.94 us
    unnamed x3 -> x0, waiting for transfers between devices: 218 us -> none
    all_to_all x1 -> x5, blocking collectives: 16.9 us -> 80 us  [exchange(): return lax.all_to_all(x, axes, split_axis=0, concat_axis=0, tiled=True)]
    psum x1 -> x0, waiting for transfers between devices: 51.5 us -> none  [on_device(): gate_part, up_part, sumsq = lax.psum((gate_part, up_part, sumsq), 'ctx')]
    all_to_all x4 -> x3, starting transfers between devices: 43.1 us -> 14.8 us  [exchange(): return lax.all_to_all(x, axes, split_axis=0, concat_axis=0, tiled=True)]
    all_to_all x4 -> x3, waiting for transfers between devices: 48.3 us -> 25.6 us  [exchange(): return lax.all_to_all(x, axes, split_axis=0, concat_axis=0, tiled=True)]
    psum x1 -> x0, blocking collectives: 12.7 us -> none  [on_device(): gate_part, up_part, sumsq = lax.psum((gate_part, up_part, sumsq), 'ctx')]
  transfers between devices with their start and end apart: 6 -> 3, of which waited for: 6 -> 3; matrix products, arithmetic and copies ran while one was open for 2% -> 0% of each run, Pallas kernels for 0% -> 0%
where the time goes in v1:
time: 147 us
  blocking collectives  80 us (54%)
  waiting for transfers between devices  25.6 us (17%)
  matrix products  15 us (10%)
  starting transfers between devices  14.8 us (10%)
  other arithmetic  5.88 us (4%)
  local copies, waits for them, and re-layouts  4.94 us (3%)
    all_to_all x5, blocking collectives, exchange(): return lax.all_to_all(x, axes, split_axis=0, concat_axis=0, tiled=True)  80 us
    all_to_all x3, waiting for transfers between devices, exchange(): return lax.all_to_all(x, axes, split_axis=0, concat_axis=0, tiled=True)  25.6 us
    all_to_all x3, starting transfers between devices, exchange(): return lax.all_to_all(x, axes, split_axis=0, concat_axis=0, tiled=True)  14.8 us
    dot_general x1, matrix products, on_device(): jnp.einsum('bhw,btw->bht', queries, latent_cache, preferred_element_type=...  5.13 us
    dot_general x1, matrix products, on_device(): jnp.einsum('bht,btl->bhl', weights.astype(BF), latent_cache[:, :, :latent...  4.37 us
  transfers between devices with their start and end apart: 3, of which 3 were waited for; matrix products, arithmetic and copies ran while one was open for 0% of the time, Pallas kernels for 0%

profile of v1, /device:TPU:1, one launch (start us, length us, event | category | flops | bytes accessed | tf_op | source)
XLA Modules:
  0.0 146.5 jit_solution(646680360685169605)
XLA Ops:
  0.0 0.9 broadcast_compare_fusion
  0.9 5.1 %select_reduce_fusion = (f32[4,128]{1,0:T(4,128)S(1)}, f32[4,128,1024]{2,1,0:T(8,128)}) fusion(pred[4,1024]{1,0:T(4,128)(4,1)S(1)} %broadcast_compare_fusion, bf16[4,128,576]{1,2,0:T(8,128)(2,1)} %param.12, bf16[4,1024,576]{1,2,0:T(8,128)(2,1)} %param.13), kind=kOutput, calls=%fused_computation.4 | convolution fusion | flops 605552128 | bytes 7411712 | tf_op jit(solution)/shard_map/bhw,btw->bht/dot_general | solution.py:49
  6.1 2.2 %fusion.8 = f32[4,128]{1,0:T(4,128)S(1)} fusion(f32[4,128,1024]{2,1,0:T(8,128)} %get-tuple-element.14, f32[4,128]{1,0:T(4,128)S(1)} %get-tuple-element.13, pred[4,1024]{1,0:T(4,128)(4,1)S(1)} %broadcast_compare_fusion), kind=kLoop, calls=%fused_computation.11 | loop fusion | flops 2096640 | bytes 2105344 | tf_op jit(solution)/shard_map/reduce_sum | solution.py:56
  8.3 4.4 %divide_convert_fusion = bf16[4,128,512]{2,1,0:T(8,128)(2,1)S(1)} fusion(bf16[4,1024,576]{1,2,0:T(8,128)(2,1)} %param.13, f32[4,128,1024]{2,1,0:T(8,128)} %get-tuple-element.14, f32[4,128]{1,0:T(4,128)S(1)} %get-tuple-element.13, pred[4,1024]{1,0:T(4,128)(4,1)S(1)} %broadcast_compare_fusion, f32[4,128]{1,0:T(4,128)S(1)} %compare_select_fusion.1), kind=kOutput, calls=%fused_computation.22 | convolution fusion | flops 539492352 | bytes 6823936 | tf_op jit(solution)/shard_map/bht,btl->bhl/dot_general | solution.py:57
  13.5 26.3 %all_to_all.40 = bf16[8,72,512]{2,1,0:T(8,128)(2,1)S(1)} all-to-all(bf16[8,72,512]{2,1,0:T(8,128)(2,1)S(1)} %pad_maximum_fusion), channel_id=1, replica_groups=mesh['ctx'=8,'row'=2,'exp'=16] {'ctx'}, dimensions={0} | all-to-all | bytes 1179648 | tf_op jit(solution)/shard_map/all_to_all | solution.py:16
  39.8 0.5 copy.88
  40.3 0.6 slice_convert_fusion
  40.9 0.9 reshape.282
  42.4 13.1 %all_to_all.41 = bf16[16,16,128]{2,1,0:T(8,128)(2,1)S(1)} all-to-all(bf16[16,16,128]{2,1,0:T(8,128)(2,1)S(1)} %reshape.275), channel_id=1, replica_groups=mesh['ctx'=8,'row'=2,'exp'=16] {'exp'}, dimensions={0} | all-to-all | bytes 131072 | tf_op jit(solution)/shard_map/all_to_all | solution.py:16
  55.6 1.4 convolution_convert_fusion
  57.0 1.3 reshape.277
  58.3 3.8 %all-to-all-start.2 = ((bf16[16,4,7168]{2,1,0:T(4,128)(2,1)}), bf16[16,4,7168]{2,1,0:T(4,128)(2,1)S(1)}, u32[]{:S(2)}, u32[]{:S(2)}) async-start(bf16[16,4,7168]{2,1,0:T(4,128)(2,1)} %reshape.277), calls=%async_computation.2 | async-start | bytes 1835008 | tf_op jit(solution)/shard_map/all_to_all | solution.py:16
  62.2 11.2 %all-to-all-done.2 = bf16[16,4,7168]{2,1,0:T(4,128)(2,1)S(1)} async-done(((bf16[16,4,7168]{2,1,0:T(4,128)(2,1)}), bf16[16,4,7168]{2,1,0:T(4,128)(2,1)S(1)}, u32[]{:S(2)}, u32[]{:S(2)}) %all-to-all-start.2) | async-done | bytes 917536 | tf_op jit(solution)/shard_map/all_to_all | solution.py:16
  73.3 1.0 reduce_sum.111
  74.3 4.9 %all-to-all-start.3 = ((bf16[8,4,896]{2,1,0:T(4,128)(2,1)}), bf16[8,4,896]{2,1,0:T(4,128)(2,1)S(1)}, u32[]{:S(2)}, u32[]{:S(2)}) async-start(bf16[8,4,896]{2,1,0:T(4,128)(2,1)} %bitcast.10), calls=%async_computation.3 | async-start | bytes 114688 | tf_op jit(solution)/shard_map/all_to_all | solution.py:16
  79.3 7.1 %all-to-all-done.3 = bf16[8,4,896]{2,1,0:T(4,128)(2,1)S(1)} async-done(((bf16[8,4,896]{2,1,0:T(4,128)(2,1)}), bf16[8,4,896]{2,1,0:T(4,128)(2,1)S(1)}, u32[]{:S(2)}, u32[]{:S(2)}) %all-to-all-start.3) | async-done | bytes 57376 | tf_op jit(solution)/shard_map/all_to_all | solution.py:16
  86.8 15.8 %all_to_all.42 = bf16[32,2,896]{2,1,0:T(2,128)(2,1)S(1)} all-to-all(bf16[32,2,896]{2,1,0:T(2,128)(2,1)S(1)} %copy.80), channel_id=1, replica_groups=mesh['ctx'=8,'row'=2,'exp'=16] {'row','exp'}, dimensions={0} | all-to-all | bytes 229376 | tf_op jit(solution)/shard_map/all_to_all | solution.py:16
  103.2 2.1 %fusion.13 = bf16[64,1024]{1,0:T(8,128)(2,1)S(1)} fusion(bf16[64,896]{1,0:T(8,128)(2,1)S(1)} %convert_element_type.250, bf16[1,896,1024]{2,1,0:T(8,128)(2,1)} %param.22), kind=kOutput, calls=%fused_computation.14 | convolution fusion | flops 117506048 | bytes 2080768 | tf_op jit(solution)/shard_map/dot_general | solution.py:102
  105.8 14.8 %all_to_all.43 = bf16[8,8,2176]{2,1,0:T(8,128)(2,1)S(1)} all-to-all(bf16[8,8,2176]{2,1,0:T(8,128)(2,1)S(1)} %fusion.32), channel_id=1, replica_groups=mesh['ctx'=8,'row'=2,'exp'=16] {'ctx'}, dimensions={0} | all-to-all | bytes 557056 | tf_op jit(solution)/shard_map/all_to_all | solution.py:16
  120.8 10.1 %all_to_all.44 = bf16[8,8,1024]{2,1,0:T(8,128)(2,1)S(1)} all-to-all(bf16[8,8,1024]{2,1,0:T(8,128)(2,1)S(1)} %broadcast_in_dim.52), channel_id=1, replica_groups=mesh['ctx'=8,'row'=2,'exp'=16] {'ctx'}, dimensions={0} | all-to-all | bytes 262144 | tf_op jit(solution)/shard_map/all_to_all | solution.py:16
  131.4 0.7 reshape.281
  132.1 6.2 %all-to-all-start.7 = ((bf16[32,2,896]{2,1,0:T(2,128)(2,1)}), bf16[32,2,896]{2,1,0:T(2,128)(2,1)S(1)}, u32[]{:S(2)}, u32[]{:S(2)}) async-start(bf16[32,2,896]{2,1,0:T(2,128)(2,1)} %reshape.281), calls=%async_computation.7 | async-start | bytes 229376 | tf_op jit(solution)/shard_map/all_to_all | solution.py:16
  138.4 7.3 %all-to-all-done.7 = bf16[32,2,896]{2,1,0:T(2,128)(2,1)S(1)} async-done(((bf16[32,2,896]{2,1,0:T(2,128)(2,1)}), bf16[32,2,896]{2,1,0:T(2,128)(2,1)S(1)}, u32[]{:S(2)}, u32[]{:S(2)}) %all-to-all-start.7) | async-done | bytes 114720 | tf_op jit(solution)/shard_map/all_to_all | solution.py:16
  145.7 0.8 fusion.20
  (61 shorter events, 3.9 us)
Async XLA Ops:
  0.0 55.6 %copy-start = (bf16[128,7168]{1,0:T(8,128)(2,1)S(1)}, bf16[128,7168]{1,0:T(8,128)(2,1)}, u32[]{:S(2)}) copy-start(bf16[128,7168]{1,0:T(8,128)(2,1)} %param.16) | copy-start | bytes 5505028
  57.0 5.1 %copy-start.3 = (s32[4,8]{1,0:T(4,128)S(1)}, s32[4,8]{1,0:T(4,128)}, u32[]{:S(2)}) copy-start(s32[4,8]{1,0:T(4,128)} %param.19) | copy-start | bytes 388
  57.0 29.4 %copy-start.4 = (bf16[4,896]{1,0:T(4,128)(2,1)S(1)}, bf16[4,896]{1,0:T(4,128)(2,1)}, u32[]{:S(2)}) copy-start(bf16[4,896]{1,0:T(4,128)(2,1)} %param.17) | copy-start | bytes 21508
  58.3 44.3 %copy-start.5 = (f32[896]{0:T(1024)S(1)}, f32[896]{0:T(1024)}, u32[]{:S(2)}) copy-start(f32[896]{0:T(1024)} %param.18) | copy-start | bytes 10756
  58.3 15.0 %all-to-all-start.2 = ((bf16[16,4,7168]{2,1,0:T(4,128)(2,1)}), bf16[16,4,7168]{2,1,0:T(4,128)(2,1)S(1)}, u32[]{:S(2)}, u32[]{:S(2)}) async-start(bf16[16,4,7168]{2,1,0:T(4,128)(2,1)} %reshape.277), calls=%async_computation.2 | async-start | bytes 1835008 | tf_op jit(solution)/shard_map/all_to_all | solution.py:16
  74.3 12.0 %all-to-all-start.3 = ((bf16[8,4,896]{2,1,0:T(4,128)(2,1)}), bf16[8,4,896]{2,1,0:T(4,128)(2,1)S(1)}, u32[]{:S(2)}, u32[]{:S(2)}) async-start(bf16[8,4,896]{2,1,0:T(4,128)(2,1)} %bitcast.10), calls=%async_computation.3 | async-start | bytes 114688 | tf_op jit(solution)/shard_map/all_to_all | solution.py:16
  103.2 2.1 %copy-start.1 = (bf16[1,896,1024]{2,1,0:T(8,128)(2,1)S(1)}, bf16[1,896,1024]{2,1,0:T(8,128)(2,1)}, u32[]{:S(2)}) copy-start(bf16[1,896,1024]{2,1,0:T(8,128)(2,1)} %param.21) | copy-start | bytes 5505028
  105.3 25.7 %copy-start.2 = (bf16[1,1024,896]{2,1,0:T(8,128)(2,1)S(1)}, bf16[1,1024,896]{2,1,0:T(8,128)(2,1)}, u32[]{:S(2)}) copy-start(bf16[1,1024,896]{2,1,0:T(8,128)(2,1)} %param.23) | copy-start | bytes 5505028
  105.8 32.5 %copy-start.6 = (f32[4,8]{1,0:T(4,128)S(1)}, f32[4,8]{1,0:T(4,128)}, u32[]{:S(2)}) copy-start(f32[4,8]{1,0:T(4,128)} %param.20) | copy-start | bytes 388
  132.1 13.6 %all-to-all-start.7 = ((bf16[32,2,896]{2,1,0:T(2,128)(2,1)}), bf16[32,2,896]{2,1,0:T(2,128)(2,1)S(1)}, u32[]{:S(2)}, u32[]{:S(2)}) async-start(bf16[32,2,896]{2,1,0:T(2,128)(2,1)} %reshape.281), calls=%async_computation.7 | async-start | bytes 229376 | tf_op jit(solution)/shard_map/all_to_all | solution.py:16

commit v2 on v1

v2 whole, which is shorter than its diff:
```python
import functools

import jax
import jax.numpy as jnp
from jax import lax
from jax.experimental import pallas as pl
from jax.experimental.pallas import tpu as pltpu
from jax.sharding import PartitionSpec as P

D = 7168
QK_HEAD = 192
BF = jnp.bfloat16
F32 = jnp.float32
I32 = jnp.int32
epsilon = 1e-06
DEAD = -1e30
MIB = 1024 * 1024


def exchange(x, axes):
    return lax.all_to_all(x, axes, split_axis=0, concat_axis=0, tiled=True)


def dot(a, b, dims=((1,), (0,))):
    return lax.dot_general(a, b, (dims, ((), ())), preferred_element_type=F32)


def iota(shape, dim):
    return lax.broadcasted_iota(I32, shape, dim)


def pieces(x):
    hi = x.astype(BF).astype(F32)
    mid = (x - hi).astype(BF).astype(F32)
    low = (x - hi - mid).astype(BF).astype(F32)
    return hi, mid, low


def call(kernel, out, args, cost, **kw):
    return pl.pallas_call(
        kernel,
        out_shape=out,
        cost_estimate=pl.CostEstimate(flops=cost[0], bytes_accessed=cost[1], transcendentals=0),
        compiler_params=pltpu.CompilerParams(vmem_limit_bytes=24 * MIB),
        **kw,
    )(*args)


def shape_of(shape, dtype):
    return jax.ShapeDtypeStruct(shape, dtype)


def attend(live_ref, q_ref, kv_ref, out_ref, stat_ref):
    r = pl.program_id(0)
    n_ctx = out_ref.shape[0]
    heads, block = q_ref.shape[1], kv_ref.shape[1]
    latent = 512
    per = heads // n_ctx
    scores = dot(q_ref[0], kv_ref[0], ((1,), (1,))) * QK_HEAD ** (-0.5)
    live = iota((heads, block), 1) < live_ref[r]
    scores = jnp.where(live, scores, DEAD)
    top = jnp.max(scores, axis=1, keepdims=True)
    weights = jnp.where(live, jnp.exp(scores - top), 0.0)
    total = jnp.sum(weights, axis=1, keepdims=True)
    safe = jnp.where(total > 0, total, 1.0)
    part = dot(weights.astype(BF), kv_ref[0, :, :latent]) * (1.0 / safe)
    part = part.astype(BF)
    lane = iota((heads, 128), 1)

    @pl.when(r == 0)
    def _():
        stat_ref[...] = jnp.zeros_like(stat_ref)

    stat = stat_ref[...]
    for p, piece in enumerate(pieces(top + jnp.log(safe))):
        stat = jnp.where(lane == 4 * r + p, piece, stat)
    stat_ref[...] = stat
    tiles = latent // 128
    base = r * tiles * per
    for c in range(n_ctx):
        for t in range(tiles):
            at = pl.multiple_of(base + t * per, per)
            out_ref[c, pl.ds(at, per), :] = part[per * c : per * (c + 1), 128 * t : 128 * (t + 1)]

    @pl.when(r == pl.num_programs(0) - 1)
    def _():
        rows = pl.num_programs(0) * tiles * per
        for c in range(n_ctx):
            out_ref[c, pl.ds(rows, per), :] = stat[per * c : per * (c + 1)].astype(BF)


def merge(got_ref, out_ref):
    n_ctx, span, _ = got_ref.shape
    per = out_ref.shape[0]
    rows = 4
    tiles = (span - per) // per // rows
    stat = got_ref[:, span - per :, :].astype(F32)
    lane = iota(stat.shape, 2)
    merged = []
    for r in range(rows):
        mine = (lane >= 4 * r) & (lane < 4 * r + 3)
        lse = jnp.sum(jnp.where(mine, stat, 0.0), axis=2, keepdims=True)
        factor = jnp.exp(lse - jnp.max(lse, axis=0, keepdims=True))
        factor = factor * (1.0 / jnp.sum(factor, axis=0, keepdims=True))
        for t in range(tiles):
            at = (r * tiles + t) * per
            merged.append(jnp.sum(factor * got_ref[:, at : at + per, :].astype(F32), axis=0))
    merged = jnp.concatenate(merged, axis=0).astype(BF)
    size = rows * tiles * per
    i, j = iota((size, size), 0), iota((size, size), 1)
    n = rows * tiles
    swap = ((i // n == j % per) & (i % n == j // per)).astype(BF)
    out_ref[...] = dot(swap, merged).astype(BF).reshape(out_ref.shape)


def project(got_ref, wv_ref, wo_ref, out_ref):
    n_exp, n, _ = got_ref.shape
    rows = 4
    tiles = n // rows
    size = n_exp * n
    count = n_exp * rows
    i, j = iota((size, size), 0), iota((size, size), 1)
    t, b = i // count, i % count
    pick = (j == (b // rows) * n + (b % rows) * tiles + t).astype(BF)
    latents = dot(pick, got_ref[...].reshape(size, 128)).astype(BF)
    values = jnp.zeros((count, wv_ref.shape[2]), F32)
    for t in range(tiles):
        values += dot(latents[count * t : count * (t + 1)], wv_ref[0, 128 * t : 128 * (t + 1), :])
    values = values.astype(BF)
    i, j = iota((2 * count, count), 0), iota((2 * count, count), 1)
    double = (j == (i // 8) * rows + i % rows).astype(BF)
    doubled = dot(double, values)
    upper = (iota(doubled.shape, 0) // rows) % 2
    lhs = jnp.concatenate(
        [jnp.where(upper == 0, doubled, 0.0), jnp.where(upper == 1, doubled, 0.0)], axis=1
    ).astype(BF)
    half = wo_ref.shape[1] // 2
    step = 512
    for at in range(0, half, step):
        rhs = jnp.concatenate([wo_ref[:, at : at + step], wo_ref[:, half + at : half + at + step]], axis=0)
        out_ref[:, :, at : at + step] = dot(lhs, rhs).astype(BF).reshape(n_exp, 8, step)


def add_heads(got_ref, out_ref):
    n_ctx, rows, width = out_ref.shape
    per = n_ctx // 2
    for q in range(per):
        total = jnp.sum(got_ref[:, :, width * q : width * (q + 1)].astype(F32), axis=0)
        out_ref[q] = total[:rows]
        out_ref[per + q] = total[rows:]


def dispatch(got_ref, stream_ref, route_ref, hidden_ref, out_ref, scratch):
    rows, width = stream_ref.shape
    hidden = (stream_ref[...].astype(F32) + jnp.sum(got_ref[...], axis=0)).astype(BF)
    hidden_ref[...] = hidden
    wide = hidden.astype(F32)
    scratch[...] = jnp.zeros_like(scratch)
    for k in range(width // 128):
        scratch[8 * k : 8 * k + rows, :] = wide[:, 128 * k : 128 * (k + 1)]
    out_ref[...] = dot(route_ref[...], scratch[...].astype(BF)).astype(BF).reshape(out_ref.shape)


def routing(ids_ref, weights_ref, route_ref, combine_ref):
    size = route_ref.shape[0]
    rows, picks = ids_ref.shape
    i, j = iota((size, 64), 0), iota((size, 64), 1)
    expert, slot = i // 16, (i // 8) % 2
    same = (i % 8) == (j // 8)
    count = jnp.zeros((size, 64), I32)
    route = jnp.zeros((size, 64), F32)
    combine = jnp.zeros((size, 64), F32)
    for b in range(rows):
        weight = jnp.zeros((size, 64), F32)
        named = jnp.zeros((size, 64), I32)
        for k in range(picks):
            hit = expert == ids_ref[b, k]
            weight = jnp.where(hit, weights_ref[b, k], weight)
            named = jnp.where(hit, 1, named)
        mine = (named == 1) & (count == slot) & same & (j % 8 == b)
        route = jnp.where(mine, 1.0, route)
        combine = jnp.where(mine, weight, combine)
        count = count + named
    route_ref[...] = route.astype(BF)
    hi = combine.astype(BF)
    low = (combine - hi.astype(F32)).astype(BF)
    combine_ref[...] = jnp.concatenate([hi, low], axis=1)


def gate_up(got_ref, gain_ref, wg_ref, wu_ref, out_ref):
    n, span, _ = got_ref.shape
    slots = n * span // 8
    tiles = wg_ref.shape[1] // 128
    i, j = iota((tiles * slots, n * span), 0), iota((tiles * slots, n * span), 1)
    pick = ((j // 8 == i % slots) & (j % 8 == i // slots)).astype(BF)
    rows = dot(pick, got_ref[...].reshape(n * span, 128))
    sumsq = jnp.zeros((slots, 128), F32)
    scaled = []
    for k in range(tiles):
        part = rows[slots * k : slots * (k + 1)]
        sumsq += part * part
        scaled.append((part * gain_ref[:, 128 * k : 128 * (k + 1)]).astype(BF))
    scaled = jnp.concatenate(scaled, axis=1)
    units = wg_ref.shape[2]
    step = 512
    per = out_ref.shape[1]
    for w_ref, base in ((wg_ref, 0), (wu_ref, units)):
        for at in range(0, units, step):
            part = dot(scaled, w_ref[0, :, at : at + step]).astype(BF)
            out_ref[:, :, base + at : base + at + step] = part.reshape(slots // per, per, step)
    lane = iota((slots, 128), 1)
    stat = jnp.zeros((slots, 128), F32)
    for p, piece in enumerate(pieces(jnp.sum(sumsq, axis=1, keepdims=True))):
        stat = jnp.where(lane == p, piece, stat)
    out_ref[:, :, 2 * units :] = stat.astype(BF).reshape(slots // per, per, 128)


def activate(got_ref, out_ref):
    units = out_ref.shape[2]
    sums = jnp.sum(got_ref[...].astype(F32), axis=0)
    sumsq = jnp.sum(sums[:, 2 * units :], axis=1, keepdims=True)
    inverse = lax.rsqrt(sumsq / D + epsilon)
    gate = inverse * sums[:, :units]
    up = inverse * sums[:, units : 2 * units]
    active = (gate / (1.0 + jnp.exp(-gate)) * up).astype(BF)
    for c in range(out_ref.shape[0]):
        out_ref[c] = active


def down(got_ref, wd_ref, out_ref):
    n_ctx, per, units = got_ref.shape
    slots = n_ctx * per
    tiles = wd_ref.shape[2] // 128
    active = got_ref[...].reshape(slots, units)
    produced = dot(active, wd_ref[0]).astype(BF)
    stacked = jnp.concatenate([produced[:, 128 * k : 128 * (k + 1)] for k in range(tiles)], axis=0)
    size = slots * 8
    i, j = iota((size, tiles * slots), 0), iota((size, tiles * slots), 1)
    place = ((i // 8 == j % slots) & (i % 8 == j // slots)).astype(BF)
    out_ref[...] = dot(place, stacked).astype(BF).reshape(out_ref.shape)


def combine_rows(got_ref, combine_ref, hidden_ref, out_ref):
    rows, width = out_ref.shape
    n, span, _ = got_ref.shape
    mixed = dot(combine_ref[...], got_ref[...].reshape(n * span, 128), ((0,), (0,)))
    mixed = mixed[:64] + mixed[64:]
    for k in range(width // 128):
        at = slice(128 * k, 128 * (k + 1))
        out_ref[:, at] = (hidden_ref[:, at].astype(F32) + mixed[8 * k : 8 * k + rows]).astype(BF)


def on_device(
    queries,
    latent_cache,
    lengths,
    w_value,
    w_out,
    stream,
    norm_gain,
    expert_ids,
    gate_weights,
    w_gate,
    w_up,
    w_down,
):
    n_ctx = lax.axis_size("ctx")
    n_row = lax.axis_size("row")
    n_exp = lax.axis_size("exp")
    groups, heads, query_width = queries.shape
    block = latent_cache.shape[1]
    latent = w_value.shape[1]
    width = stream.shape[1]
    units = w_gate.shape[2]
    experts = n_row * n_exp
    slots = 2 * experts
    per = heads // n_ctx
    tiles = latent // 128
    span = groups * tiles * per + per

    route, combine = call(
        routing,
        (shape_of((slots * 8, 64), BF), shape_of((slots * 8, 128), BF)),
        (expert_ids, gate_weights),
        (slots * 8 * 64 * 100, slots * 8 * 400),
        in_specs=[pl.BlockSpec(memory_space=pltpu.SMEM)] * 2,
    )
    live = jnp.clip(lengths - lax.axis_index("ctx") * block, 0, block)
    sent = pl.pallas_call(
        attend,
        out_shape=shape_of((n_ctx, span, 128), BF),
        grid=(groups,),
        in_specs=[
            pl.BlockSpec(memory_space=pltpu.SMEM),
            pl.BlockSpec((1, heads, query_width), lambda r: (r, 0, 0)),
            pl.BlockSpec((1, block, query_width), lambda r: (r, 0, 0)),
        ],
        out_specs=pl.BlockSpec((n_ctx, span, 128), lambda r: (0, 0, 0)),
        scratch_shapes=[pltpu.VMEM((heads, 128), F32)],
        cost_estimate=pl.CostEstimate(
            flops=2 * groups * heads * block * (query_width + latent),
            bytes_accessed=2 * groups * (block + heads) * query_width,
            transcendentals=groups * heads * block,
        ),
        compiler_params=pltpu.CompilerParams(vmem_limit_bytes=24 * MIB),
    )(live, queries, latent_cache)
    got = exchange(sent, "ctx")
    sent = call(merge, shape_of((n_exp, groups * tiles, 128), BF), (got,), (1 << 22, 1 << 20))
    got = exchange(sent, "exp")
    sent = call(
        project,
        shape_of((n_exp, 2 * groups, D // 2), BF),
        (got, w_value, w_out),
        (2 * 128 * 256 * D // 2, 2 * 128 * D * 2),
    )
    got = exchange(sent, "exp")
    sent = call(add_heads, shape_of((n_ctx, groups, width), F32), (got,), (1 << 20, 1 << 20))
    got = exchange(sent, "ctx")
    hidden, sent = call(
        dispatch,
        (shape_of((groups, width), BF), shape_of((experts, 16, 128), BF)),
        (got, stream, route),
        (1 << 23, 1 << 19),
        scratch_shapes=[pltpu.VMEM((64, 128), F32)],
    )
    got = exchange(sent, ("row", "exp"))
    sent = call(
        gate_up,
        shape_of((n_ctx, slots // n_ctx, 2 * units + 128), BF),
        (got, norm_gain.reshape(1, width), w_gate, w_up),
        (4 * slots * width * units, 4 * width * units),
    )
    got = exchange(sent, "ctx")
    sent = call(activate, shape_of((n_ctx, slots // n_ctx, units), BF), (got,), (1 << 20, 1 << 19))
    got = exchange(sent, "ctx")
    sent = call(
        down,
        shape_of((experts, 16, 128), BF),
        (got, w_down),
        (2 * slots * width * units, 2 * width * units),
    )
    got = exchange(sent, ("row", "exp"))
    return call(
        combine_rows, shape_of((groups, width), BF), (got, combine, hidden), (1 << 24, 1 << 18)
    )


def solution(mesh):
    placed = (
        P(("row", "exp"), None, None),
        P(("row", "exp"), "ctx", None),
        P(("row", "exp")),
        P(("ctx", "exp"), None, None),
        P(("ctx", "exp"), None),
        P(("row", "exp"), "ctx"),
        P("ctx"),
        P(("row", "exp"), None),
        P(("row", "exp"), None),
        P(("row", "exp"), "ctx", None),
        P(("row", "exp"), "ctx", None),
        P(("row", "exp"), None, "ctx"),
    )
    return jax.shard_map(
        on_device, mesh=mesh, in_specs=placed, out_specs=P(("row", "exp"), "ctx"), check_vma=False
    )
```

time: 147 us -> 144 us (0.980)
  matrix products: 15 us -> 0 us
  waiting for transfers between devices: 25.6 us -> 13.5 us
  Pallas kernels: 0 us -> 11.9 us
  blocking collectives: 80 us -> 90.7 us
  local copies, waits for them, and re-layouts: 4.94 us -> 13.1 us
  other arithmetic: 5.88 us -> 0.01 us
    dot_general x8 -> x0, matrix products: 15 us -> none  [the longest x1 5.13 us: on_device(): jnp.einsum('bhw,btw->bht', queries, latent_cache, preferred_element_type=...]
    unnamed x14 -> x24, local copies, waits for them, and re-layouts: 0.04 us -> 13.1 us
    all_to_all x3 -> x2, waiting for transfers between devices: 25.6 us -> 13.5 us  [exchange(): return lax.all_to_all(x, axes, split_axis=0, concat_axis=0, tiled=True)]
    pallas_call x0 -> x10, Pallas kernels: none -> 11.9 us  [the longest x9 7.45 us: call(): pl.pallas_call(kernel, out_shape=out, cost_estimate=pl.CostEstimate(flops...]
    all_to_all x5 -> x6, blocking collectives: 80 us -> 90.7 us  [exchange(): return lax.all_to_all(x, axes, split_axis=0, concat_axis=0, tiled=True)]
    reduce_sum x10 -> x0, other arithmetic: 3.86 us -> none  [the longest x1 2.17 us: on_device(): totals = jnp.sum(weights, axis=2)]
    reshape x8 -> x1, local copies, waits for them, and re-layouts: 2.9 us -> 0.01 us  [on_device(): norm_gain.reshape(1, width)]
    all_to_all x3 -> x2, starting transfers between devices: 14.8 us -> 14.2 us  [exchange(): return lax.all_to_all(x, axes, split_axis=0, concat_axis=0, tiled=True)]
  transfers between devices with their start and end apart: 3 -> 2, of which waited for: 3 -> 2; matrix products, arithmetic and copies ran while one was open for 0% -> 0% of each run, Pallas kernels for 0% -> 1%
where the time goes in v2:
time: 144 us
  blocking collectives  90.7 us (63%)
  starting transfers between devices  14.2 us (10%)
  waiting for transfers between devices  13.5 us (9%)
  local copies, waits for them, and re-layouts  13.1 us (9%)
  Pallas kernels  11.9 us (8%)
    all_to_all x6, blocking collectives, exchange(): return lax.all_to_all(x, axes, split_axis=0, concat_axis=0, tiled=True)  90.7 us
    all_to_all x2, starting transfers between devices, exchange(): return lax.all_to_all(x, axes, split_axis=0, concat_axis=0, tiled=True)  14.2 us
    all_to_all x2, waiting for transfers between devices, exchange(): return lax.all_to_all(x, axes, split_axis=0, concat_axis=0, tiled=True)  13.5 us
    unnamed x24, local copies, waits for them, and re-layouts  13.1 us
    pallas_call x9, Pallas kernels, call(): pl.pallas_call(kernel, out_shape=out, cost_estimate=pl.CostEstimate(flops...  7.45 us
    pallas_call x1, Pallas kernels, on_device(): pl.pallas_call(attend, out_shape=shape_of((n_ctx, span, 128), BF), grid=(...  4.49 us
  transfers between devices with their start and end apart: 2, of which 2 were waited for; matrix products, arithmetic and copies ran while one was open for 0% of the time, Pallas kernels for 1%

profile of v2, /device:TPU:1, one launch (start us, length us, event | category | flops | bytes accessed | tf_op | source)
XLA Modules:
  0.0 143.6 jit_solution(11798054797598734339)
XLA Ops:
  0.0 1.4 copy.13.q_ref
  1.4 7.7 %copy.14.kv_ref = bf16[4,1024,576]{2,1,0:T(8,128)(2,1)} copy(bf16[4,1024,576]{1,2,0:T(8,128)(2,1)} %param.13) | data formatting | bytes 9437184 | tf_op args[1]
  9.1 2.5 %copy-done = bf16[4,1024,576]{2,1,0:T(8,128)(2,1)S(1)} copy-done((bf16[4,1024,576]{2,1,0:T(8,128)(2,1)S(1)}, bf16[4,1024,576]{2,1,0:T(8,128)(2,1)}, u32[]{:S(2)}) %copy-start) | copy-done | bytes 4718616
  11.6 4.5 %shard_map.118 = bf16[8,272,128]{2,1,0:T(8,128)(2,1)S(1)} custom-call(s32[4]{0:T(128)S(1)} %subtract_clamp_fusion.live_ref, bf16[4,128,576]{2,1,0:T(8,128)(2,1)S(1)} %copy.13.q_ref, bf16[4,1024,576]{2,1,0:T(8,128)(2,1)S(1)} %copy-done), custom_call_target="tpu_custom_call" | custom-call | flops 1140850688 | bytes 5308416 | tf_op jit(solution)/shard_map/pallas_call | solution.py:289
  16.1 25.4 %all_to_all.40.got_ref = bf16[8,272,128]{2,1,0:T(8,128)(2,1)S(1)} all-to-all(bf16[8,272,128]{2,1,0:T(8,128)(2,1)S(1)} %shard_map.118), channel_id=1, replica_groups=mesh['ctx'=8,'row'=2,'exp'=16] {'ctx'}, dimensions={0} | all-to-all | bytes 1114112 | tf_op jit(solution)/shard_map/all_to_all | solution.py:21
  41.4 0.4 shard_map.119
  41.8 13.1 %all_to_all.41.got_ref = bf16[16,16,128]{2,1,0:T(8,128)(2,1)S(1)} all-to-all(bf16[16,16,128]{2,1,0:T(8,128)(2,1)S(1)} %shard_map.119), channel_id=1, replica_groups=mesh['ctx'=8,'row'=2,'exp'=16] {'exp'}, dimensions={0} | all-to-all | bytes 131072 | tf_op jit(solution)/shard_map/all_to_all | solution.py:21
  55.0 0.8 shard_map.120
  55.9 13.9 %all_to_all.42.got_ref = bf16[16,8,3584]{2,1,0:T(8,128)(2,1)S(1)} all-to-all(bf16[16,8,3584]{2,1,0:T(8,128)(2,1)S(1)} %shard_map.120), channel_id=1, replica_groups=mesh['ctx'=8,'row'=2,'exp'=16] {'exp'}, dimensions={0} | all-to-all | bytes 1835008 | tf_op jit(solution)/shard_map/all_to_all | solution.py:21
  69.8 0.8 shard_map.121
  70.6 5.4 %all-to-all-start.3 = ((f32[8,4,896]{2,1,0:T(4,128)}), f32[8,4,896]{2,1,0:T(4,128)S(1)}, u32[]{:S(2)}, u32[]{:S(2)}) async-start(f32[8,4,896]{2,1,0:T(4,128)} %shard_map.121), calls=%async_computation.3 | async-start | bytes 229376 | tf_op jit(solution)/shard_map/all_to_all | solution.py:21
  76.0 1.8 %shard_map.122 = (bf16[512,64]{1,0:T(8,128)(2,1)S(1)}, bf16[512,128]{1,0:T(8,128)(2,1)S(1)}) custom-call(s32[4,8]{1,0:T(4,128)S(1)} %copy-done.7, f32[4,8]{1,0:T(4,128)S(1)} %copy-done.8), custom_call_target="tpu_custom_call" | custom-call | flops 3276800 | bytes 204800 | tf_op jit(solution)/shard_map/pallas_call | solution.py:40
  77.8 5.9 %all-to-all-done.3.got_ref = f32[8,4,896]{2,1,0:T(4,128)S(1)} async-done(((f32[8,4,896]{2,1,0:T(4,128)}), f32[8,4,896]{2,1,0:T(4,128)S(1)}, u32[]{:S(2)}, u32[]{:S(2)}) %all-to-all-start.3) | async-done | bytes 114720 | tf_op jit(solution)/shard_map/all_to_all | solution.py:21
  83.7 0.9 shard_map.123
  84.6 8.8 %all-to-all-start.4 = ((bf16[32,16,128]{2,1,0:T(8,128)(2,1)}), bf16[32,16,128]{2,1,0:T(8,128)(2,1)S(1)}, u32[]{:S(2)}, u32[]{:S(2)}) async-start(bf16[32,16,128]{2,1,0:T(8,128)(2,1)} %get-tuple-element.10), calls=%async_computation.4 | async-start | bytes 262144 | tf_op jit(solution)/shard_map/all_to_all | solution.py:21
  93.4 7.5 %all-to-all-done.4.got_ref = bf16[32,16,128]{2,1,0:T(8,128)(2,1)S(1)} async-done(((bf16[32,16,128]{2,1,0:T(8,128)(2,1)}), bf16[32,16,128]{2,1,0:T(8,128)(2,1)S(1)}, u32[]{:S(2)}, u32[]{:S(2)}) %all-to-all-start.4) | async-done | bytes 131104 | tf_op jit(solution)/shard_map/all_to_all | solution.py:21
  101.0 1.5 %copy-done.2 = bf16[1,896,1024]{2,1,0:T(8,128)(2,1)S(1)} copy-done((bf16[1,896,1024]{2,1,0:T(8,128)(2,1)S(1)}, bf16[1,896,1024]{2,1,0:T(8,128)(2,1)}, u32[]{:S(2)}) %copy-start.2) | copy-done | bytes 1835032
  102.5 1.1 shard_map.124
  103.6 14.4 %all_to_all.43.got_ref = bf16[8,8,2176]{2,1,0:T(8,128)(2,1)S(1)} all-to-all(bf16[8,8,2176]{2,1,0:T(8,128)(2,1)S(1)} %shard_map.124), channel_id=1, replica_groups=mesh['ctx'=8,'row'=2,'exp'=16] {'ctx'}, dimensions={0} | all-to-all | bytes 557056 | tf_op jit(solution)/shard_map/all_to_all | solution.py:21
  118.0 0.1 shard_map.125
  118.1 10.3 %all_to_all.44.got_ref = bf16[8,8,1024]{2,1,0:T(8,128)(2,1)S(1)} all-to-all(bf16[8,8,1024]{2,1,0:T(8,128)(2,1)S(1)} %shard_map.125), channel_id=1, replica_groups=mesh['ctx'=8,'row'=2,'exp'=16] {'ctx'}, dimensions={0} | all-to-all | bytes 262144 | tf_op jit(solution)/shard_map/all_to_all | solution.py:21
  128.4 0.7 shard_map.126
  129.1 13.6 %all_to_all.45.got_ref = bf16[32,16,128]{2,1,0:T(8,128)(2,1)S(1)} all-to-all(bf16[32,16,128]{2,1,0:T(8,128)(2,1)S(1)} %shard_map.126), channel_id=1, replica_groups=mesh['ctx'=8,'row'=2,'exp'=16] {'row','exp'}, dimensions={0} | all-to-all | bytes 262144 | tf_op jit(solution)/shard_map/all_to_all | solution.py:21
  142.7 0.8 shard_map.127
  (22 shorter events, 0.1 us)
Async XLA Ops:
  1.4 7.7 %copy-start.10 = (s32[4]{0:T(128)S(1)}, s32[4]{0:T(128)}, u32[]{:S(2)}) copy-start(s32[4]{0:T(128)} %param.14) | copy-start | bytes 52
  9.1 2.5 %copy-start = (bf16[4,1024,576]{2,1,0:T(8,128)(2,1)S(1)}, bf16[4,1024,576]{2,1,0:T(8,128)(2,1)}, u32[]{:S(2)}) copy-start(bf16[4,1024,576]{2,1,0:T(8,128)(2,1)} %copy.14.kv_ref) | copy-start | bytes 14155780
  11.5 43.4 %copy-start.5 = (bf16[1,512,128]{2,1,0:T(8,128)(2,1)S(1)}, bf16[1,512,128]{2,1,0:T(8,128)(2,1)}, u32[]{:S(2)}) copy-start(bf16[1,512,128]{2,1,0:T(8,128)(2,1)} %wv_ref.1) | copy-start | bytes 393220
  16.0 38.9 %copy-start.3 = (bf16[128,7168]{1,0:T(8,128)(2,1)S(1)}, bf16[128,7168]{1,0:T(8,128)(2,1)}, u32[]{:S(2)}) copy-start(bf16[128,7168]{1,0:T(8,128)(2,1)} %wo_ref.1) | copy-start | bytes 5505028
  55.8 20.2 %copy-start.7 = (s32[4,8]{1,0:T(4,128)S(1)}, s32[4,8]{1,0:T(4,128)}, u32[]{:S(2)}) copy-start(s32[4,8]{1,0:T(4,128)} %ids_ref.1) | copy-start | bytes 388
  55.8 20.1 %copy-start.8 = (f32[4,8]{1,0:T(4,128)S(1)}, f32[4,8]{1,0:T(4,128)}, u32[]{:S(2)}) copy-start(f32[4,8]{1,0:T(4,128)} %weights_ref.1) | copy-start | bytes 388
  55.9 27.9 %copy-start.6 = (bf16[4,896]{1,0:T(4,128)(2,1)S(1)}, bf16[4,896]{1,0:T(4,128)(2,1)}, u32[]{:S(2)}) copy-start(bf16[4,896]{1,0:T(4,128)(2,1)} %stream_ref.1) | copy-start | bytes 21508
  55.9 37.5 %copy-start.9 = (f32[896]{0:T(1024)S(1)}, f32[896]{0:T(1024)}, u32[]{:S(2)}) copy-start(f32[896]{0:T(1024)} %param.18) | copy-start | bytes 10756
  55.9 45.1 %copy-start.1 = (bf16[1,896,1024]{2,1,0:T(8,128)(2,1)S(1)}, bf16[1,896,1024]{2,1,0:T(8,128)(2,1)}, u32[]{:S(2)}) copy-start(bf16[1,896,1024]{2,1,0:T(8,128)(2,1)} %wg_ref.1) | copy-start | bytes 5505028
  70.6 13.2 %all-to-all-start.3 = ((f32[8,4,896]{2,1,0:T(4,128)}), f32[8,4,896]{2,1,0:T(4,128)S(1)}, u32[]{:S(2)}, u32[]{:S(2)}) async-start(f32[8,4,896]{2,1,0:T(4,128)} %shard_map.121), calls=%async_computation.3 | async-start | bytes 229376 | tf_op jit(solution)/shard_map/all_to_all | solution.py:21
  84.6 16.3 %all-to-all-start.4 = ((bf16[32,16,128]{2,1,0:T(8,128)(2,1)}), bf16[32,16,128]{2,1,0:T(8,128)(2,1)S(1)}, u32[]{:S(2)}, u32[]{:S(2)}) async-start(bf16[32,16,128]{2,1,0:T(8,128)(2,1)} %get-tuple-element.10), calls=%async_computation.4 | async-start | bytes 262144 | tf_op jit(solution)/shard_map/all_to_all | solution.py:21
  101.0 1.5 %copy-start.2 = (bf16[1,896,1024]{2,1,0:T(8,128)(2,1)S(1)}, bf16[1,896,1024]{2,1,0:T(8,128)(2,1)}, u32[]{:S(2)}) copy-start(bf16[1,896,1024]{2,1,0:T(8,128)(2,1)} %wu_ref.1) | copy-start | bytes 5505028
  102.5 26.0 %copy-start.4 = (bf16[1,1024,896]{2,1,0:T(8,128)(2,1)S(1)}, bf16[1,1024,896]{2,1,0:T(8,128)(2,1)}, u32[]{:S(2)}) copy-start(bf16[1,1024,896]{2,1,0:T(8,128)(2,1)} %wd_ref.1) | copy-start | bytes 5505028

commit v3 on v2

--- a/solution.py
+++ b/solution.py
@@ -53,17 +53,17 @@
 def attend(live_ref, q_ref, kv_ref, out_ref, stat_ref):
     r = pl.program_id(0)
     n_ctx = out_ref.shape[0]
-    heads, block = q_ref.shape[1], kv_ref.shape[1]
+    heads, block = q_ref.shape[2], kv_ref.shape[2]
     latent = 512
     per = heads // n_ctx
-    scores = dot(q_ref[0], kv_ref[0], ((1,), (1,))) * QK_HEAD ** (-0.5)
+    scores = dot(q_ref[0], kv_ref[0], ((0,), (0,))) * QK_HEAD ** (-0.5)
     live = iota((heads, block), 1) < live_ref[r]
     scores = jnp.where(live, scores, DEAD)
     top = jnp.max(scores, axis=1, keepdims=True)
     weights = jnp.where(live, jnp.exp(scores - top), 0.0)
     total = jnp.sum(weights, axis=1, keepdims=True)
     safe = jnp.where(total > 0, total, 1.0)
-    part = dot(weights.astype(BF), kv_ref[0, :, :latent]) * (1.0 / safe)
+    part = dot(weights.astype(BF), kv_ref[0, :latent, :], ((1,), (1,))) * (1.0 / safe)
     part = part.astype(BF)
     lane = iota((heads, 128), 1)
 
@@ -292,8 +292,8 @@
         grid=(groups,),
         in_specs=[
             pl.BlockSpec(memory_space=pltpu.SMEM),
-            pl.BlockSpec((1, heads, query_width), lambda r: (r, 0, 0)),
-            pl.BlockSpec((1, block, query_width), lambda r: (r, 0, 0)),
+            pl.BlockSpec((1, query_width, heads), lambda r: (r, 0, 0)),
+            pl.BlockSpec((1, query_width, block), lambda r: (r, 0, 0)),
         ],
         out_specs=pl.BlockSpec((n_ctx, span, 128), lambda r: (0, 0, 0)),
         scratch_shapes=[pltpu.VMEM((heads, 128), F32)],
@@ -303,7 +303,7 @@
             transcendentals=groups * heads * block,
         ),
         compiler_params=pltpu.CompilerParams(vmem_limit_bytes=24 * MIB),
-    )(live, queries, latent_cache)
+    )(live, jnp.swapaxes(queries, 1, 2), jnp.swapaxes(latent_cache, 1, 2))
     got = exchange(sent, "ctx")
     sent = call(merge, shape_of((n_exp, groups * tiles, 128), BF), (got,), (1 << 22, 1 << 20))
     got = exchange(sent, "exp")

time: 144 us -> 137 us (0.951)
  local copies, waits for them, and re-layouts: 13.1 us -> 4.95 us
    unnamed x24 -> x22, local copies, waits for them, and re-layouts: 13.1 us -> 4.95 us
where the time goes in v3:
time: 137 us; the launch traced here: 136 us
  blocking collectives  90.6 us (66%)
  starting transfers between devices  14.3 us (10%)
  waiting for transfers between devices  13.5 us (10%)
  Pallas kernels  11.9 us (9%)
  local copies, waits for them, and re-layouts  4.95 us (4%)
    all_to_all x6, blocking collectives, exchange(): return lax.all_to_all(x, axes, split_axis=0, concat_axis=0, tiled=True)  90.6 us
    all_to_all x2, starting transfers between devices, exchange(): return lax.all_to_all(x, axes, split_axis=0, concat_axis=0, tiled=True)  14.3 us
    all_to_all x2, waiting for transfers between devices, exchange(): return lax.all_to_all(x, axes, split_axis=0, concat_axis=0, tiled=True)  13.5 us
    pallas_call x9, Pallas kernels, call(): pl.pallas_call(kernel, out_shape=out, cost_estimate=pl.CostEstimate(flops...  7.49 us
    unnamed x22, local copies, waits for them, and re-layouts  4.95 us
    pallas_call x1, Pallas kernels, on_device(): pl.pallas_call(attend, out_shape=shape_of((n_ctx, span, 128), BF), grid=(...  4.38 us
  transfers between devices with their start and end apart: 2, of which 2 were waited for; matrix products, arithmetic and copies ran while one was open for 0% of the time, Pallas kernels for 1%

profile of v3, /device:TPU:1, one launch (start us, length us, event | category | flops | bytes accessed | tf_op | source)
XLA Modules:
  0.0 136.0 jit_solution(2547753043931400323)
XLA Ops:
  0.0 0.7 subtract_clamp_fusion.live_ref
  0.7 2.3 %copy-done = bf16[4,1024,576]{1,2,0:T(8,128)(2,1)S(1)} copy-done((bf16[4,1024,576]{1,2,0:T(8,128)(2,1)S(1)}, bf16[4,1024,576]{1,2,0:T(8,128)(2,1)}, u32[]{:S(2)}) %copy-start) | copy-done | bytes 4718616
  3.0 1.1 copy-done.5
  4.1 4.4 %shard_map.118 = bf16[8,272,128]{2,1,0:T(8,128)(2,1)S(1)} custom-call(s32[4]{0:T(128)S(1)} %subtract_clamp_fusion.live_ref, bf16[4,576,128]{2,1,0:T(8,128)(2,1)S(1)} %bitcast.3, bf16[4,576,1024]{2,1,0:T(8,128)(2,1)S(1)} %bitcast.2), custom_call_target="tpu_custom_call" | custom-call | flops 1140850688 | bytes 5308416 | tf_op jit(solution)/shard_map/pallas_call | solution.py:289
  8.5 25.4 %all_to_all.40.got_ref = bf16[8,272,128]{2,1,0:T(8,128)(2,1)S(1)} all-to-all(bf16[8,272,128]{2,1,0:T(8,128)(2,1)S(1)} %shard_map.118), channel_id=1, replica_groups=mesh['ctx'=8,'row'=2,'exp'=16] {'ctx'}, dimensions={0} | all-to-all | bytes 1114112 | tf_op jit(solution)/shard_map/all_to_all | solution.py:21
  33.9 0.4 shard_map.119
  34.3 13.0 %all_to_all.41.got_ref = bf16[16,16,128]{2,1,0:T(8,128)(2,1)S(1)} all-to-all(bf16[16,16,128]{2,1,0:T(8,128)(2,1)S(1)} %shard_map.119), channel_id=1, replica_groups=mesh['ctx'=8,'row'=2,'exp'=16] {'exp'}, dimensions={0} | all-to-all | bytes 131072 | tf_op jit(solution)/shard_map/all_to_all | solution.py:21
  47.3 0.8 shard_map.120
  48.2 13.9 %all_to_all.42.got_ref = bf16[16,8,3584]{2,1,0:T(8,128)(2,1)S(1)} all-to-all(bf16[16,8,3584]{2,1,0:T(8,128)(2,1)S(1)} %shard_map.120), channel_id=1, replica_groups=mesh['ctx'=8,'row'=2,'exp'=16] {'exp'}, dimensions={0} | all-to-all | bytes 1835008 | tf_op jit(solution)/shard_map/all_to_all | solution.py:21
  62.1 0.8 shard_map.121
  62.9 5.5 %all-to-all-start.3 = ((f32[8,4,896]{2,1,0:T(4,128)}), f32[8,4,896]{2,1,0:T(4,128)S(1)}, u32[]{:S(2)}, u32[]{:S(2)}) async-start(f32[8,4,896]{2,1,0:T(4,128)} %shard_map.121), calls=%async_computation.3 | async-start | bytes 229376 | tf_op jit(solution)/shard_map/all_to_all | solution.py:21
  68.4 1.8 %shard_map.122 = (bf16[512,64]{1,0:T(8,128)(2,1)S(1)}, bf16[512,128]{1,0:T(8,128)(2,1)S(1)}) custom-call(s32[4,8]{1,0:T(4,128)S(1)} %copy-done.8, f32[4,8]{1,0:T(4,128)S(1)} %copy-done.9), custom_call_target="tpu_custom_call" | custom-call | flops 3276800 | bytes 204800 | tf_op jit(solution)/shard_map/pallas_call | solution.py:40
  70.2 5.9 %all-to-all-done.3.got_ref = f32[8,4,896]{2,1,0:T(4,128)S(1)} async-done(((f32[8,4,896]{2,1,0:T(4,128)}), f32[8,4,896]{2,1,0:T(4,128)S(1)}, u32[]{:S(2)}, u32[]{:S(2)}) %all-to-all-start.3) | async-done | bytes 114720 | tf_op jit(solution)/shard_map/all_to_all | solution.py:21
  76.2 0.9 shard_map.123
  77.0 8.8 %all-to-all-start.4 = ((bf16[32,16,128]{2,1,0:T(8,128)(2,1)}), bf16[32,16,128]{2,1,0:T(8,128)(2,1)S(1)}, u32[]{:S(2)}, u32[]{:S(2)}) async-start(bf16[32,16,128]{2,1,0:T(8,128)(2,1)} %get-tuple-element.10), calls=%async_computation.4 | async-start | bytes 262144 | tf_op jit(solution)/shard_map/all_to_all | solution.py:21
  85.9 7.5 %all-to-all-done.4.got_ref = bf16[32,16,128]{2,1,0:T(8,128)(2,1)S(1)} async-done(((bf16[32,16,128]{2,1,0:T(8,128)(2,1)}), bf16[32,16,128]{2,1,0:T(8,128)(2,1)S(1)}, u32[]{:S(2)}, u32[]{:S(2)}) %all-to-all-start.4) | async-done | bytes 131104 | tf_op jit(solution)/shard_map/all_to_all | solution.py:21
  93.4 1.5 %copy-done.2 = bf16[1,896,1024]{2,1,0:T(8,128)(2,1)S(1)} copy-done((bf16[1,896,1024]{2,1,0:T(8,128)(2,1)S(1)}, bf16[1,896,1024]{2,1,0:T(8,128)(2,1)}, u32[]{:S(2)}) %copy-start.2) | copy-done | bytes 1835032
  94.9 1.2 shard_map.124
  96.0 14.4 %all_to_all.43.got_ref = bf16[8,8,2176]{2,1,0:T(8,128)(2,1)S(1)} all-to-all(bf16[8,8,2176]{2,1,0:T(8,128)(2,1)S(1)} %shard_map.124), channel_id=1, replica_groups=mesh['ctx'=8,'row'=2,'exp'=16] {'ctx'}, dimensions={0} | all-to-all | bytes 557056 | tf_op jit(solution)/shard_map/all_to_all | solution.py:21
  110.4 0.1 shard_map.125
  110.5 10.3 %all_to_all.44.got_ref = bf16[8,8,1024]{2,1,0:T(8,128)(2,1)S(1)} all-to-all(bf16[8,8,1024]{2,1,0:T(8,128)(2,1)S(1)} %shard_map.125), channel_id=1, replica_groups=mesh['ctx'=8,'row'=2,'exp'=16] {'ctx'}, dimensions={0} | all-to-all | bytes 262144 | tf_op jit(solution)/shard_map/all_to_all | solution.py:21
  120.9 0.7 shard_map.126
  121.6 13.6 %all_to_all.45.got_ref = bf16[32,16,128]{2,1,0:T(8,128)(2,1)S(1)} all-to-all(bf16[32,16,128]{2,1,0:T(8,128)(2,1)S(1)} %shard_map.126), channel_id=1, replica_groups=mesh['ctx'=8,'row'=2,'exp'=16] {'row','exp'}, dimensions={0} | all-to-all | bytes 262144 | tf_op jit(solution)/shard_map/all_to_all | solution.py:21
  135.2 0.8 shard_map.127
  (20 shorter events, 0.1 us)
Async XLA Ops:
  0.7 2.3 %copy-start = (bf16[4,1024,576]{1,2,0:T(8,128)(2,1)S(1)}, bf16[4,1024,576]{1,2,0:T(8,128)(2,1)}, u32[]{:S(2)}) copy-start(bf16[4,1024,576]{1,2,0:T(8,128)(2,1)} %param.13) | copy-start | bytes 14155780
  3.0 1.1 copy-start.5
  4.1 43.3 %copy-start.6 = (bf16[1,512,128]{2,1,0:T(8,128)(2,1)S(1)}, bf16[1,512,128]{2,1,0:T(8,128)(2,1)}, u32[]{:S(2)}) copy-start(bf16[1,512,128]{2,1,0:T(8,128)(2,1)} %wv_ref.1) | copy-start | bytes 393220
  8.5 38.9 %copy-start.3 = (bf16[128,7168]{1,0:T(8,128)(2,1)S(1)}, bf16[128,7168]{1,0:T(8,128)(2,1)}, u32[]{:S(2)}) copy-start(bf16[128,7168]{1,0:T(8,128)(2,1)} %wo_ref.1) | copy-start | bytes 5505028
  48.2 20.2 %copy-start.8 = (s32[4,8]{1,0:T(4,128)S(1)}, s32[4,8]{1,0:T(4,128)}, u32[]{:S(2)}) copy-start(s32[4,8]{1,0:T(4,128)} %ids_ref.1) | copy-start | bytes 388
  48.2 20.2 %copy-start.9 = (f32[4,8]{1,0:T(4,128)S(1)}, f32[4,8]{1,0:T(4,128)}, u32[]{:S(2)}) copy-start(f32[4,8]{1,0:T(4,128)} %weights_ref.1) | copy-start | bytes 388
  48.2 28.0 %copy-start.7 = (bf16[4,896]{1,0:T(4,128)(2,1)S(1)}, bf16[4,896]{1,0:T(4,128)(2,1)}, u32[]{:S(2)}) copy-start(bf16[4,896]{1,0:T(4,128)(2,1)} %stream_ref.1) | copy-start | bytes 21508
  48.2 37.6 %copy-start.10 = (f32[896]{0:T(1024)S(1)}, f32[896]{0:T(1024)}, u32[]{:S(2)}) copy-start(f32[896]{0:T(1024)} %param.18) | copy-start | bytes 10756
  48.2 45.1 %copy-start.1 = (bf16[1,896,1024]{2,1,0:T(8,128)(2,1)S(1)}, bf16[1,896,1024]{2,1,0:T(8,128)(2,1)}, u32[]{:S(2)}) copy-start(bf16[1,896,1024]{2,1,0:T(8,128)(2,1)} %wg_ref.1) | copy-start | bytes 5505028
  62.9 13.3 %all-to-all-start.3 = ((f32[8,4,896]{2,1,0:T(4,128)}), f32[8,4,896]{2,1,0:T(4,128)S(1)}, u32[]{:S(2)}, u32[]{:S(2)}) async-start(f32[8,4,896]{2,1,0:T(4,128)} %shard_map.121), calls=%async_computation.3 | async-start | bytes 229376 | tf_op jit(solution)/shard_map/all_to_all | solution.py:21
  77.0 16.3 %all-to-all-start.4 = ((bf16[32,16,128]{2,1,0:T(8,128)(2,1)}), bf16[32,16,128]{2,1,0:T(8,128)(2,1)S(1)}, u32[]{:S(2)}, u32[]{:S(2)}) async-start(bf16[32,16,128]{2,1,0:T(8,128)(2,1)} %get-tuple-element.10), calls=%async_computation.4 | async-start | bytes 262144 | tf_op jit(solution)/shard_map/all_to_all | solution.py:21
  93.4 1.5 %copy-start.2 = (bf16[1,896,1024]{2,1,0:T(8,128)(2,1)S(1)}, bf16[1,896,1024]{2,1,0:T(8,128)(2,1)}, u32[]{:S(2)}) copy-start(bf16[1,896,1024]{2,1,0:T(8,128)(2,1)} %wu_ref.1) | copy-start | bytes 5505028
  94.9 26.0 %copy-start.4 = (bf16[1,1024,896]{2,1,0:T(8,128)(2,1)S(1)}, bf16[1,1024,896]{2,1,0:T(8,128)(2,1)}, u32[]{:S(2)}) copy-start(bf16[1,1024,896]{2,1,0:T(8,128)(2,1)} %wd_ref.1) | copy-start | bytes 5505028

commit v4 on v3

--- a/solution.py
+++ b/solution.py
@@ -50,43 +50,49 @@
     return jax.ShapeDtypeStruct(shape, dtype)
 
 
-def attend(live_ref, q_ref, kv_ref, out_ref, stat_ref):
-    r = pl.program_id(0)
-    n_ctx = out_ref.shape[0]
-    heads, block = q_ref.shape[2], kv_ref.shape[2]
-    latent = 512
+def attend(length_hbm, q_hbm, kv_hbm, out_ref, q_ref, kv_ref, length_ref, sem, length_sem):
+    rows, _, heads = q_ref.shape
+    block = kv_ref.shape[2]
+    n_ctx, span, _ = out_ref.shape
     per = heads // n_ctx
-    scores = dot(q_ref[0], kv_ref[0], ((0,), (0,))) * QK_HEAD ** (-0.5)
-    live = iota((heads, block), 1) < live_ref[r]
-    scores = jnp.where(live, scores, DEAD)
-    top = jnp.max(scores, axis=1, keepdims=True)
-    weights = jnp.where(live, jnp.exp(scores - top), 0.0)
-    total = jnp.sum(weights, axis=1, keepdims=True)
-    safe = jnp.where(total > 0, total, 1.0)
-    part = dot(weights.astype(BF), kv_ref[0, :latent, :], ((1,), (1,))) * (1.0 / safe)
-    part = part.astype(BF)
+    tiles = (span - per) // per // rows
+    latent = tiles * 128
+    copies = []
+    for r in range(rows):
+        pair = (
+            pltpu.make_async_copy(q_hbm.at[r], q_ref.at[r], sem.at[0, r]),
+            pltpu.make_async_copy(kv_hbm.at[r], kv_ref.at[r], sem.at[1, r]),
+        )
+        for copy in pair:
+            copy.start()
+        copies.append(pair)
+    length_copy = pltpu.make_async_copy(length_hbm, length_ref, length_sem)
+    length_copy.start()
+    length_copy.wait()
+    first = lax.axis_index("ctx") * block
     lane = iota((heads, 128), 1)
-
-    @pl.when(r == 0)
-    def _():
-        stat_ref[...] = jnp.zeros_like(stat_ref)
-
-    stat = stat_ref[...]
-    for p, piece in enumerate(pieces(top + jnp.log(safe))):
-        stat = jnp.where(lane == 4 * r + p, piece, stat)
-    stat_ref[...] = stat
-    tiles = latent // 128
-    base = r * tiles * per
+    stat = jnp.zeros((heads, 128), F32)
+    for r in range(rows):
+        for copy in copies[r]:
+            copy.wait()
+        scores = dot(q_ref[r], kv_ref[r], ((0,), (0,))) * QK_HEAD ** (-0.5)
+        live = iota((heads, block), 1) < length_ref[r] - first
+        scores = jnp.where(live, scores, DEAD)
+        top = jnp.max(scores, axis=1, keepdims=True)
+        weights = jnp.where(live, jnp.exp(scores - top), 0.0)
+        total = jnp.sum(weights, axis=1, keepdims=True)
+        safe = jnp.where(total > 0, total, 1.0)
+        part = dot(weights.astype(BF), kv_ref[r, :latent, :], ((1,), (1,))) * (1.0 / safe)
+        part = part.astype(BF)
+        for p, piece in enumerate(pieces(top + jnp.log(safe))):
+            stat = jnp.where(lane == 4 * r + p, piece, stat)
+        for c in range(n_ctx):
+            for t in range(tiles):
+                at = (r * tiles + t) * per
+                out_ref[c, at : at + per, :] = part[per * c : per * (c + 1), 128 * t : 128 * (t + 1)]
+    stat = stat.astype(BF)
     for c in range(n_ctx):
-        for t in range(tiles):
-            at = pl.multiple_of(base + t * per, per)
-            out_ref[c, pl.ds(at, per), :] = part[per * c : per * (c + 1), 128 * t : 128 * (t + 1)]
-
-    @pl.when(r == pl.num_programs(0) - 1)
-    def _():
-        rows = pl.num_programs(0) * tiles * per
-        for c in range(n_ctx):
-            out_ref[c, pl.ds(rows, per), :] = stat[per * c : per * (c + 1)].astype(BF)
+        out_ref[c, span - per :, :] = stat[per * c : per * (c + 1)]
 
 
 def merge(got_ref, out_ref):
@@ -146,13 +152,13 @@
     per = n_ctx // 2
     for q in range(per):
         total = jnp.sum(got_ref[:, :, width * q : width * (q + 1)].astype(F32), axis=0)
-        out_ref[q] = total[:rows]
-        out_ref[per + q] = total[rows:]
+        out_ref[q] = total[:rows].astype(BF)
+        out_ref[per + q] = total[rows:].astype(BF)
 
 
 def dispatch(got_ref, stream_ref, route_ref, hidden_ref, out_ref, scratch):
     rows, width = stream_ref.shape
-    hidden = (stream_ref[...].astype(F32) + jnp.sum(got_ref[...], axis=0)).astype(BF)
+    hidden = (stream_ref[...].astype(F32) + jnp.sum(got_ref[...].astype(F32), axis=0)).astype(BF)
     hidden_ref[...] = hidden
     wide = hidden.astype(F32)
     scratch[...] = jnp.zeros_like(scratch)
@@ -285,25 +291,28 @@
         (slots * 8 * 64 * 100, slots * 8 * 400),
         in_specs=[pl.BlockSpec(memory_space=pltpu.SMEM)] * 2,
     )
-    live = jnp.clip(lengths - lax.axis_index("ctx") * block, 0, block)
     sent = pl.pallas_call(
         attend,
         out_shape=shape_of((n_ctx, span, 128), BF),
-        grid=(groups,),
         in_specs=[
-            pl.BlockSpec(memory_space=pltpu.SMEM),
-            pl.BlockSpec((1, query_width, heads), lambda r: (r, 0, 0)),
-            pl.BlockSpec((1, query_width, block), lambda r: (r, 0, 0)),
+            pl.BlockSpec(memory_space=pltpu.HBM),
+            pl.BlockSpec(memory_space=pltpu.HBM),
+            pl.BlockSpec(memory_space=pltpu.HBM),
         ],
-        out_specs=pl.BlockSpec((n_ctx, span, 128), lambda r: (0, 0, 0)),
-        scratch_shapes=[pltpu.VMEM((heads, 128), F32)],
+        scratch_shapes=[
+            pltpu.VMEM((groups, query_width, heads), BF),
+            pltpu.VMEM((groups, query_width, block), BF),
+            pltpu.SMEM((groups,), I32),
+            pltpu.SemaphoreType.DMA((2, groups)),
+            pltpu.SemaphoreType.DMA,
+        ],
         cost_estimate=pl.CostEstimate(
             flops=2 * groups * heads * block * (query_width + latent),
             bytes_accessed=2 * groups * (block + heads) * query_width,
             transcendentals=groups * heads * block,
         ),
-        compiler_params=pltpu.CompilerParams(vmem_limit_bytes=24 * MIB),
-    )(live, jnp.swapaxes(queries, 1, 2), jnp.swapaxes(latent_cache, 1, 2))
+        compiler_params=pltpu.CompilerParams(vmem_limit_bytes=53 * MIB),
+    )(lengths, jnp.swapaxes(queries, 1, 2), jnp.swapaxes(latent_cache, 1, 2))
     got = exchange(sent, "ctx")
     sent = call(merge, shape_of((n_exp, groups * tiles, 128), BF), (got,), (1 << 22, 1 << 20))
     got = exchange(sent, "exp")
@@ -314,7 +323,7 @@
         (2 * 128 * 256 * D // 2, 2 * 128 * D * 2),
     )
     got = exchange(sent, "exp")
-    sent = call(add_heads, shape_of((n_ctx, groups, width), F32), (got,), (1 << 20, 1 << 20))
+    sent = call(add_heads, shape_of((n_ctx, groups, width), BF), (got,), (1 << 20, 1 << 20))
     got = exchange(sent, "ctx")
     hidden, sent = call(
         dispatch,

time: 137 us -> 133 us (0.971)
  local copies, waits for them, and re-layouts: 4.95 us -> 2.2 us
    unnamed x22 -> x20, local copies, waits for them, and re-layouts: 4.95 us -> 2.2 us
where the time goes in v4:
time: 133 us
  blocking collectives  90.7 us (68%)
  starting transfers between devices  14.3 us (11%)
  waiting for transfers between devices  12.8 us (10%)
  Pallas kernels  12.5 us (9%)
  local copies, waits for them, and re-layouts  2.2 us (2%)
    all_to_all x6, blocking collectives, exchange(): return lax.all_to_all(x, axes, split_axis=0, concat_axis=0, tiled=True)  90.7 us
    all_to_all x2, starting transfers between devices, exchange(): return lax.all_to_all(x, axes, split_axis=0, concat_axis=0, tiled=True)  14.3 us
    all_to_all x2, waiting for transfers between devices, exchange(): return lax.all_to_all(x, axes, split_axis=0, concat_axis=0, tiled=True)  12.8 us
    pallas_call x9, Pallas kernels, call(): pl.pallas_call(kernel, out_shape=out, cost_estimate=pl.CostEstimate(flops...  7.47 us
    pallas_call x1, Pallas kernels, on_device(): pl.pallas_call(attend, out_shape=shape_of((n_ctx, span, 128), BF), in_spe...  5.06 us
  transfers between devices with their start and end apart: 2, of which 2 were waited for; matrix products, arithmetic and copies ran while one was open for 0% of the time, Pallas kernels for 1%

profile of v4, /device:TPU:1, one launch (start us, length us, event | category | flops | bytes accessed | tf_op | source)
XLA Modules:
  0.0 132.7 jit_solution(17115801623874779091)
XLA Ops:
  0.0 0.7 copy-done.6
  0.7 5.1 %shard_map.118 = bf16[8,272,128]{2,1,0:T(8,128)(2,1)S(1)} custom-call(s32[4]{0:T(128)S(1)} %copy-done.6, bf16[4,576,128]{2,1,0:T(8,128)(2,1)} %bitcast.3, bf16[4,576,1024]{2,1,0:T(8,128)(2,1)} %bitcast.2), custom_call_target="tpu_custom_call" | custom-call | flops 1140850688 | bytes 5308416 | tf_op jit(solution)/shard_map/pallas_call | solution.py:294
  5.7 0.0 copy-start.2
  5.7 25.4 %all_to_all.40.got_ref = bf16[8,272,128]{2,1,0:T(8,128)(2,1)S(1)} all-to-all(bf16[8,272,128]{2,1,0:T(8,128)(2,1)S(1)} %shard_map.118), channel_id=1, replica_groups=mesh['ctx'=8,'row'=2,'exp'=16] {'ctx'}, dimensions={0} | all-to-all | bytes 1114112 | tf_op jit(solution)/shard_map/all_to_all | solution.py:21
  31.1 0.4 shard_map.119
  31.5 13.1 %all_to_all.41.got_ref = bf16[16,16,128]{2,1,0:T(8,128)(2,1)S(1)} all-to-all(bf16[16,16,128]{2,1,0:T(8,128)(2,1)S(1)} %shard_map.119), channel_id=1, replica_groups=mesh['ctx'=8,'row'=2,'exp'=16] {'exp'}, dimensions={0} | all-to-all | bytes 131072 | tf_op jit(solution)/shard_map/all_to_all | solution.py:21
  44.7 0.8 shard_map.120
  45.5 0.0 copy-start.7
  45.6 13.9 %all_to_all.42.got_ref = bf16[16,8,3584]{2,1,0:T(8,128)(2,1)S(1)} all-to-all(bf16[16,8,3584]{2,1,0:T(8,128)(2,1)S(1)} %shard_map.120), channel_id=1, replica_groups=mesh['ctx'=8,'row'=2,'exp'=16] {'exp'}, dimensions={0} | all-to-all | bytes 1835008 | tf_op jit(solution)/shard_map/all_to_all | solution.py:21
  59.5 0.7 shard_map.121
  60.2 5.5 %all-to-all-start.3 = ((bf16[8,4,896]{2,1,0:T(4,128)(2,1)}), bf16[8,4,896]{2,1,0:T(4,128)(2,1)S(1)}, u32[]{:S(2)}, u32[]{:S(2)}) async-start(bf16[8,4,896]{2,1,0:T(4,128)(2,1)} %shard_map.121), calls=%async_computation.3 | async-start | bytes 114688 | tf_op jit(solution)/shard_map/all_to_all | solution.py:21
  65.7 1.8 %shard_map.122 = (bf16[512,64]{1,0:T(8,128)(2,1)S(1)}, bf16[512,128]{1,0:T(8,128)(2,1)S(1)}) custom-call(s32[4,8]{1,0:T(4,128)S(1)} %copy-done.7, f32[4,8]{1,0:T(4,128)S(1)} %copy-done.8), custom_call_target="tpu_custom_call" | custom-call | flops 3276800 | bytes 204800 | tf_op jit(solution)/shard_map/pallas_call | solution.py:40
  67.5 5.3 %all-to-all-done.3.got_ref = bf16[8,4,896]{2,1,0:T(4,128)(2,1)S(1)} async-done(((bf16[8,4,896]{2,1,0:T(4,128)(2,1)}), bf16[8,4,896]{2,1,0:T(4,128)(2,1)S(1)}, u32[]{:S(2)}, u32[]{:S(2)}) %all-to-all-start.3) | async-done | bytes 57376 | tf_op jit(solution)/shard_map/all_to_all | solution.py:21
  72.8 0.9 shard_map.123
  73.7 8.8 %all-to-all-start.4 = ((bf16[32,16,128]{2,1,0:T(8,128)(2,1)}), bf16[32,16,128]{2,1,0:T(8,128)(2,1)S(1)}, u32[]{:S(2)}, u32[]{:S(2)}) async-start(bf16[32,16,128]{2,1,0:T(8,128)(2,1)} %get-tuple-element.10), calls=%async_computation.4 | async-start | bytes 262144 | tf_op jit(solution)/shard_map/all_to_all | solution.py:21
  82.5 7.5 %all-to-all-done.4.got_ref = bf16[32,16,128]{2,1,0:T(8,128)(2,1)S(1)} async-done(((bf16[32,16,128]{2,1,0:T(8,128)(2,1)}), bf16[32,16,128]{2,1,0:T(8,128)(2,1)S(1)}, u32[]{:S(2)}, u32[]{:S(2)}) %all-to-all-start.4) | async-done | bytes 131104 | tf_op jit(solution)/shard_map/all_to_all | solution.py:21
  90.0 1.5 %copy-done.1 = bf16[1,896,1024]{2,1,0:T(8,128)(2,1)S(1)} copy-done((bf16[1,896,1024]{2,1,0:T(8,128)(2,1)S(1)}, bf16[1,896,1024]{2,1,0:T(8,128)(2,1)}, u32[]{:S(2)}) %copy-start.1) | copy-done | bytes 1835032
  91.5 1.2 shard_map.124
  92.7 14.4 %all_to_all.43.got_ref = bf16[8,8,2176]{2,1,0:T(8,128)(2,1)S(1)} all-to-all(bf16[8,8,2176]{2,1,0:T(8,128)(2,1)S(1)} %shard_map.124), channel_id=1, replica_groups=mesh['ctx'=8,'row'=2,'exp'=16] {'ctx'}, dimensions={0} | all-to-all | bytes 557056 | tf_op jit(solution)/shard_map/all_to_all | solution.py:21
  107.1 0.1 shard_map.125
  107.2 10.3 %all_to_all.44.got_ref = bf16[8,8,1024]{2,1,0:T(8,128)(2,1)S(1)} all-to-all(bf16[8,8,1024]{2,1,0:T(8,128)(2,1)S(1)} %shard_map.125), channel_id=1, replica_groups=mesh['ctx'=8,'row'=2,'exp'=16] {'ctx'}, dimensions={0} | all-to-all | bytes 262144 | tf_op jit(solution)/shard_map/all_to_all | solution.py:21
  117.5 0.7 shard_map.126
  118.2 13.6 %all_to_all.45.got_ref = bf16[32,16,128]{2,1,0:T(8,128)(2,1)S(1)} all-to-all(bf16[32,16,128]{2,1,0:T(8,128)(2,1)S(1)} %shard_map.126), channel_id=1, replica_groups=mesh['ctx'=8,'row'=2,'exp'=16] {'row','exp'}, dimensions={0} | all-to-all | bytes 262144 | tf_op jit(solution)/shard_map/all_to_all | solution.py:21
  131.8 0.8 shard_map.127
  (17 shorter events, 0.0 us)
Async XLA Ops:
  0.0 0.7 copy-start.6
  0.7 44.0 %copy-start.4 = (bf16[1,512,128]{2,1,0:T(8,128)(2,1)S(1)}, bf16[1,512,128]{2,1,0:T(8,128)(2,1)}, u32[]{:S(2)}) copy-start(bf16[1,512,128]{2,1,0:T(8,128)(2,1)} %wv_ref.1) | copy-start | bytes 393220
  5.7 38.9 %copy-start.2 = (bf16[128,7168]{1,0:T(8,128)(2,1)S(1)}, bf16[128,7168]{1,0:T(8,128)(2,1)}, u32[]{:S(2)}) copy-start(bf16[128,7168]{1,0:T(8,128)(2,1)} %wo_ref.1) | copy-start | bytes 5505028
  45.5 20.2 %copy-start.7 = (s32[4,8]{1,0:T(4,128)S(1)}, s32[4,8]{1,0:T(4,128)}, u32[]{:S(2)}) copy-start(s32[4,8]{1,0:T(4,128)} %ids_ref.1) | copy-start | bytes 388
  45.5 20.2 %copy-start.8 = (f32[4,8]{1,0:T(4,128)S(1)}, f32[4,8]{1,0:T(4,128)}, u32[]{:S(2)}) copy-start(f32[4,8]{1,0:T(4,128)} %weights_ref.1) | copy-start | bytes 388
  45.5 27.3 %copy-start.5 = (bf16[4,896]{1,0:T(4,128)(2,1)S(1)}, bf16[4,896]{1,0:T(4,128)(2,1)}, u32[]{:S(2)}) copy-start(bf16[4,896]{1,0:T(4,128)(2,1)} %stream_ref.1) | copy-start | bytes 21508
  45.5 36.9 %copy-start.9 = (f32[896]{0:T(1024)S(1)}, f32[896]{0:T(1024)}, u32[]{:S(2)}) copy-start(f32[896]{0:T(1024)} %param.18) | copy-start | bytes 10756
  45.6 44.4 %copy-start = (bf16[1,896,1024]{2,1,0:T(8,128)(2,1)S(1)}, bf16[1,896,1024]{2,1,0:T(8,128)(2,1)}, u32[]{:S(2)}) copy-start(bf16[1,896,1024]{2,1,0:T(8,128)(2,1)} %wg_ref.1) | copy-start | bytes 5505028
  60.2 12.6 %all-to-all-start.3 = ((bf16[8,4,896]{2,1,0:T(4,128)(2,1)}), bf16[8,4,896]{2,1,0:T(4,128)(2,1)S(1)}, u32[]{:S(2)}, u32[]{:S(2)}) async-start(bf16[8,4,896]{2,1,0:T(4,128)(2,1)} %shard_map.121), calls=%async_computation.3 | async-start | bytes 114688 | tf_op jit(solution)/shard_map/all_to_all | solution.py:21
  73.7 16.3 %all-to-all-start.4 = ((bf16[32,16,128]{2,1,0:T(8,128)(2,1)}), bf16[32,16,128]{2,1,0:T(8,128)(2,1)S(1)}, u32[]{:S(2)}, u32[]{:S(2)}) async-start(bf16[32,16,128]{2,1,0:T(8,128)(2,1)} %get-tuple-element.10), calls=%async_computation.4 | async-start | bytes 262144 | tf_op jit(solution)/shard_map/all_to_all | solution.py:21
  90.0 1.5 %copy-start.1 = (bf16[1,896,1024]{2,1,0:T(8,128)(2,1)S(1)}, bf16[1,896,1024]{2,1,0:T(8,128)(2,1)}, u32[]{:S(2)}) copy-start(bf16[1,896,1024]{2,1,0:T(8,128)(2,1)} %wu_ref.1) | copy-start | bytes 5505028
  91.5 26.0 %copy-start.3 = (bf16[1,1024,896]{2,1,0:T(8,128)(2,1)S(1)}, bf16[1,1024,896]{2,1,0:T(8,128)(2,1)}, u32[]{:S(2)}) copy-start(bf16[1,1024,896]{2,1,0:T(8,128)(2,1)} %wd_ref.1) | copy-start | bytes 5505028

commit v5 on v4

--- a/solution.py
+++ b/solution.py
@@ -156,7 +156,8 @@
         out_ref[per + q] = total[rows:].astype(BF)
 
 
-def dispatch(got_ref, stream_ref, route_ref, hidden_ref, out_ref, scratch):
+def dispatch(got_ref, stream_ref, route_ref, gain_ref, later_ref, hidden_ref, out_ref, scratch):
+    del gain_ref, later_ref
     rows, width = stream_ref.shape
     hidden = (stream_ref[...].astype(F32) + jnp.sum(got_ref[...].astype(F32), axis=0)).astype(BF)
     hidden_ref[...] = hidden
@@ -284,6 +285,9 @@
     tiles = latent // 128
     span = groups * tiles * per + per
 
+    vmem = pl.BlockSpec(memory_space=pltpu.VMEM)
+    anywhere = pl.BlockSpec(memory_space=pl.ANY)
+    gain = norm_gain.reshape(1, width)
     route, combine = call(
         routing,
         (shape_of((slots * 8, 64), BF), shape_of((slots * 8, 128), BF)),
@@ -328,15 +332,16 @@
     hidden, sent = call(
         dispatch,
         (shape_of((groups, width), BF), shape_of((experts, 16, 128), BF)),
-        (got, stream, route),
+        (got, stream, route, gain, w_up),
         (1 << 23, 1 << 19),
+        in_specs=[vmem] * 3 + [anywhere] * 2,
         scratch_shapes=[pltpu.VMEM((64, 128), F32)],
     )
     got = exchange(sent, ("row", "exp"))
     sent = call(
         gate_up,
         shape_of((n_ctx, slots // n_ctx, 2 * units + 128), BF),
-        (got, norm_gain.reshape(1, width), w_gate, w_up),
+        (got, gain, w_gate, w_up),
         (4 * slots * width * units, 4 * width * units),
     )
     got = exchange(sent, "ctx")

time: 133 us -> 131 us (0.985)
  blocking collectives: 90.7 us -> 107 us
  starting transfers between devices: 14.3 us -> 5.47 us
  waiting for transfers between devices: 12.8 us -> 5.31 us
  local copies, waits for them, and re-layouts: 2.2 us -> 0.71 us
    all_to_all x6 -> x7, blocking collectives: 90.7 us -> 107 us  [exchange(): return lax.all_to_all(x, axes, split_axis=0, concat_axis=0, tiled=True)]
    all_to_all x2 -> x1, starting transfers between devices: 14.3 us -> 5.47 us  [exchange(): return lax.all_to_all(x, axes, split_axis=0, concat_axis=0, tiled=True)]
    all_to_all x2 -> x1, waiting for transfers between devices: 12.8 us -> 5.31 us  [exchange(): return lax.all_to_all(x, axes, split_axis=0, concat_axis=0, tiled=True)]
    unnamed x20, local copies, waits for them, and re-layouts: 2.2 us -> 0.7 us
  transfers between devices with their start and end apart: 2 -> 1, of which waited for: 2 -> 1; matrix products, arithmetic and copies ran while one was open for 0% -> 0% of each run, Pallas kernels for 1% -> 1%
where the time goes in v5:
time: 131 us; the launch traced here: 130 us
  blocking collectives  107 us (82%)
  Pallas kernels  11.8 us (9%)
  starting transfers between devices  5.47 us (4%)
  waiting for transfers between devices  5.31 us (4%)
    all_to_all x7, blocking collectives, exchange(): return lax.all_to_all(x, axes, split_axis=0, concat_axis=0, tiled=True)  107 us
    pallas_call x9, Pallas kernels, call(): pl.pallas_call(kernel, out_shape=out, cost_estimate=pl.CostEstimate(flops...  6.76 us
    all_to_all x1, starting transfers between devices, exchange(): return lax.all_to_all(x, axes, split_axis=0, concat_axis=0, tiled=True)  5.47 us
    all_to_all x1, waiting for transfers between devices, exchange(): return lax.all_to_all(x, axes, split_axis=0, concat_axis=0, tiled=True)  5.31 us
    pallas_call x1, Pallas kernels, on_device(): pl.pallas_call(attend, out_shape=shape_of((n_ctx, span, 128), BF), in_spe...  5.06 us
  transfers between devices with their start and end apart: 1, of which 1 were waited for; matrix products, arithmetic and copies ran while one was open for 0% of the time, Pallas kernels for 1%

profile of v5, /device:TPU:1, one launch (start us, length us, event | category | flops | bytes accessed | tf_op | source)
XLA Modules:
  0.0 130.4 jit_solution(14234588611840717541)
XLA Ops:
  0.0 0.7 copy-done.6
  0.7 5.1 %shard_map.118 = bf16[8,272,128]{2,1,0:T(8,128)(2,1)S(1)} custom-call(s32[4]{0:T(128)S(1)} %copy-done.6, bf16[4,576,128]{2,1,0:T(8,128)(2,1)} %bitcast.3, bf16[4,576,1024]{2,1,0:T(8,128)(2,1)} %bitcast.2), custom_call_target="tpu_custom_call" | custom-call | flops 1140850688 | bytes 5308416 | tf_op jit(solution)/shard_map/pallas_call | solution.py:298
  5.7 0.0 copy-start.2
  5.7 25.4 %all_to_all.40.got_ref = bf16[8,272,128]{2,1,0:T(8,128)(2,1)S(1)} all-to-all(bf16[8,272,128]{2,1,0:T(8,128)(2,1)S(1)} %shard_map.118), channel_id=1, replica_groups=mesh['ctx'=8,'row'=2,'exp'=16] {'ctx'}, dimensions={0} | all-to-all | bytes 1114112 | tf_op jit(solution)/shard_map/all_to_all | solution.py:21
  31.1 0.4 shard_map.119
  31.5 13.1 %all_to_all.41.got_ref = bf16[16,16,128]{2,1,0:T(8,128)(2,1)S(1)} all-to-all(bf16[16,16,128]{2,1,0:T(8,128)(2,1)S(1)} %shard_map.119), channel_id=1, replica_groups=mesh['ctx'=8,'row'=2,'exp'=16] {'exp'}, dimensions={0} | all-to-all | bytes 131072 | tf_op jit(solution)/shard_map/all_to_all | solution.py:21
  44.7 0.8 shard_map.120
  45.5 0.0 copy-start.9
  45.5 0.0 copy-start.7
  45.5 0.0 copy-start.8
  45.6 13.9 %all_to_all.42.got_ref = bf16[16,8,3584]{2,1,0:T(8,128)(2,1)S(1)} all-to-all(bf16[16,8,3584]{2,1,0:T(8,128)(2,1)S(1)} %shard_map.120), channel_id=1, replica_groups=mesh['ctx'=8,'row'=2,'exp'=16] {'exp'}, dimensions={0} | all-to-all | bytes 1835008 | tf_op jit(solution)/shard_map/all_to_all | solution.py:21
  59.5 0.8 shard_map.121
  60.2 5.5 %all-to-all-start.3 = ((bf16[8,4,896]{2,1,0:T(4,128)(2,1)}), bf16[8,4,896]{2,1,0:T(4,128)(2,1)S(1)}, u32[]{:S(2)}, u32[]{:S(2)}) async-start(bf16[8,4,896]{2,1,0:T(4,128)(2,1)} %shard_map.121), calls=%async_computation.3 | async-start | bytes 114688 | tf_op jit(solution)/shard_map/all_to_all | solution.py:21
  65.7 1.8 %shard_map.122 = (bf16[512,64]{1,0:T(8,128)(2,1)S(1)}, bf16[512,128]{1,0:T(8,128)(2,1)S(1)}) custom-call(s32[4,8]{1,0:T(4,128)S(1)} %copy-done.7, f32[4,8]{1,0:T(4,128)S(1)} %copy-done.8), custom_call_target="tpu_custom_call" | custom-call | flops 3276800 | bytes 204800 | tf_op jit(solution)/shard_map/pallas_call | solution.py:40
  67.5 5.3 %all-to-all-done.3.got_ref = bf16[8,4,896]{2,1,0:T(4,128)(2,1)S(1)} async-done(((bf16[8,4,896]{2,1,0:T(4,128)(2,1)}), bf16[8,4,896]{2,1,0:T(4,128)(2,1)S(1)}, u32[]{:S(2)}, u32[]{:S(2)}) %all-to-all-start.3) | async-done | bytes 57376 | tf_op jit(solution)/shard_map/all_to_all | solution.py:21
  72.8 0.2 shard_map.123
  73.0 16.2 %all_to_all.43.got_ref = bf16[32,16,128]{2,1,0:T(8,128)(2,1)S(1)} all-to-all(bf16[32,16,128]{2,1,0:T(8,128)(2,1)S(1)} %get-tuple-element.10), channel_id=1, replica_groups=mesh['ctx'=8,'row'=2,'exp'=16] {'row','exp'}, dimensions={0} | all-to-all | bytes 262144 | tf_op jit(solution)/shard_map/all_to_all | solution.py:21
  89.3 1.1 shard_map.124
  90.4 14.4 %all_to_all.44.got_ref = bf16[8,8,2176]{2,1,0:T(8,128)(2,1)S(1)} all-to-all(bf16[8,8,2176]{2,1,0:T(8,128)(2,1)S(1)} %shard_map.124), channel_id=1, replica_groups=mesh['ctx'=8,'row'=2,'exp'=16] {'ctx'}, dimensions={0} | all-to-all | bytes 557056 | tf_op jit(solution)/shard_map/all_to_all | solution.py:21
  104.8 0.1 shard_map.125
  104.9 10.3 %all_to_all.45.got_ref = bf16[8,8,1024]{2,1,0:T(8,128)(2,1)S(1)} all-to-all(bf16[8,8,1024]{2,1,0:T(8,128)(2,1)S(1)} %shard_map.125), channel_id=1, replica_groups=mesh['ctx'=8,'row'=2,'exp'=16] {'ctx'}, dimensions={0} | all-to-all | bytes 262144 | tf_op jit(solution)/shard_map/all_to_all | solution.py:21
  115.2 0.7 shard_map.126
  116.0 13.6 %all_to_all.46.got_ref = bf16[32,16,128]{2,1,0:T(8,128)(2,1)S(1)} all-to-all(bf16[32,16,128]{2,1,0:T(8,128)(2,1)S(1)} %shard_map.126), channel_id=1, replica_groups=mesh['ctx'=8,'row'=2,'exp'=16] {'row','exp'}, dimensions={0} | all-to-all | bytes 262144 | tf_op jit(solution)/shard_map/all_to_all | solution.py:21
  129.6 0.8 shard_map.127
  (16 shorter events, 0.0 us)
Async XLA Ops:
  0.0 0.7 copy-start.6
  0.7 44.0 %copy-start.4 = (bf16[1,512,128]{2,1,0:T(8,128)(2,1)S(1)}, bf16[1,512,128]{2,1,0:T(8,128)(2,1)}, u32[]{:S(2)}) copy-start(bf16[1,512,128]{2,1,0:T(8,128)(2,1)} %wv_ref.1) | copy-start | bytes 393220
  5.7 38.9 %copy-start.2 = (bf16[128,7168]{1,0:T(8,128)(2,1)S(1)}, bf16[128,7168]{1,0:T(8,128)(2,1)}, u32[]{:S(2)}) copy-start(bf16[128,7168]{1,0:T(8,128)(2,1)} %wo_ref.1) | copy-start | bytes 5505028
  45.5 20.2 %copy-start.9 = (f32[896]{0:T(1024)S(1)}, f32[896]{0:T(1024)}, u32[]{:S(2)}) copy-start(f32[896]{0:T(1024)} %param.18) | copy-start | bytes 10756
  45.5 20.2 %copy-start.7 = (s32[4,8]{1,0:T(4,128)S(1)}, s32[4,8]{1,0:T(4,128)}, u32[]{:S(2)}) copy-start(s32[4,8]{1,0:T(4,128)} %ids_ref.1) | copy-start | bytes 388
  45.5 20.2 %copy-start.8 = (f32[4,8]{1,0:T(4,128)S(1)}, f32[4,8]{1,0:T(4,128)}, u32[]{:S(2)}) copy-start(f32[4,8]{1,0:T(4,128)} %weights_ref.1) | copy-start | bytes 388
  45.5 27.3 %copy-start = (bf16[1,896,1024]{2,1,0:T(8,128)(2,1)S(1)}, bf16[1,896,1024]{2,1,0:T(8,128)(2,1)}, u32[]{:S(2)}) copy-start(bf16[1,896,1024]{2,1,0:T(8,128)(2,1)} %wu_ref.1) | copy-start | bytes 5505028
  45.6 27.3 %copy-start.5 = (bf16[4,896]{1,0:T(4,128)(2,1)S(1)}, bf16[4,896]{1,0:T(4,128)(2,1)}, u32[]{:S(2)}) copy-start(bf16[4,896]{1,0:T(4,128)(2,1)} %stream_ref.1) | copy-start | bytes 21508
  60.2 12.6 %all-to-all-start.3 = ((bf16[8,4,896]{2,1,0:T(4,128)(2,1)}), bf16[8,4,896]{2,1,0:T(4,128)(2,1)S(1)}, u32[]{:S(2)}, u32[]{:S(2)}) async-start(bf16[8,4,896]{2,1,0:T(4,128)(2,1)} %shard_map.121), calls=%async_computation.3 | async-start | bytes 114688 | tf_op jit(solution)/shard_map/all_to_all | solution.py:21
  72.8 16.5 %copy-start.1 = (bf16[1,896,1024]{2,1,0:T(8,128)(2,1)S(1)}, bf16[1,896,1024]{2,1,0:T(8,128)(2,1)}, u32[]{:S(2)}) copy-start(bf16[1,896,1024]{2,1,0:T(8,128)(2,1)} %wg_ref.1) | copy-start | bytes 5505028
  89.3 26.0 %copy-start.3 = (bf16[1,1024,896]{2,1,0:T(8,128)(2,1)S(1)}, bf16[1,1024,896]{2,1,0:T(8,128)(2,1)}, u32[]{:S(2)}) copy-start(bf16[1,1024,896]{2,1,0:T(8,128)(2,1)} %wd_ref.1) | copy-start | bytes 5505028

commit v6 on v5

--- a/solution.py
+++ b/solution.py
@@ -95,51 +95,45 @@
         out_ref[c, span - per :, :] = stat[per * c : per * (c + 1)]
 
 
-def merge(got_ref, out_ref):
+def merge(got_ref, out_ref, scratch):
     n_ctx, span, _ = got_ref.shape
     per = out_ref.shape[0]
     rows = 4
     tiles = (span - per) // per // rows
     stat = got_ref[:, span - per :, :].astype(F32)
     lane = iota(stat.shape, 2)
-    merged = []
+    n = rows * tiles
     for r in range(rows):
         mine = (lane >= 4 * r) & (lane < 4 * r + 3)
         lse = jnp.sum(jnp.where(mine, stat, 0.0), axis=2, keepdims=True)
         factor = jnp.exp(lse - jnp.max(lse, axis=0, keepdims=True))
         factor = factor * (1.0 / jnp.sum(factor, axis=0, keepdims=True))
         for t in range(tiles):
-            at = (r * tiles + t) * per
-            merged.append(jnp.sum(factor * got_ref[:, at : at + per, :].astype(F32), axis=0))
-    merged = jnp.concatenate(merged, axis=0).astype(BF)
-    size = rows * tiles * per
-    i, j = iota((size, size), 0), iota((size, size), 1)
-    n = rows * tiles
-    swap = ((i // n == j % per) & (i % n == j // per)).astype(BF)
-    out_ref[...] = dot(swap, merged).astype(BF).reshape(out_ref.shape)
-
-
-def project(got_ref, wv_ref, wo_ref, out_ref):
+            at = r * tiles + t
+            part = got_ref[:, at * per : (at + 1) * per, :].astype(F32)
+            scratch[pl.ds(at, per, stride=n), :] = jnp.sum(factor * part, axis=0)
+    out_ref[...] = scratch[...].astype(BF).reshape(out_ref.shape)
+
+
+def project(got_ref, wv_ref, wo_ref, out_ref, got_wide, values_wide, upper, lower):
     n_exp, n, _ = got_ref.shape
     rows = 4
     tiles = n // rows
     size = n_exp * n
     count = n_exp * rows
-    i, j = iota((size, size), 0), iota((size, size), 1)
-    t, b = i // count, i % count
-    pick = (j == (b // rows) * n + (b % rows) * tiles + t).astype(BF)
-    latents = dot(pick, got_ref[...].reshape(size, 128)).astype(BF)
+    got_wide[...] = got_ref[...].astype(F32).reshape(size, 128)
     values = jnp.zeros((count, wv_ref.shape[2]), F32)
     for t in range(tiles):
-        values += dot(latents[count * t : count * (t + 1)], wv_ref[0, 128 * t : 128 * (t + 1), :])
-    values = values.astype(BF)
-    i, j = iota((2 * count, count), 0), iota((2 * count, count), 1)
-    double = (j == (i // 8) * rows + i % rows).astype(BF)
-    doubled = dot(double, values)
-    upper = (iota(doubled.shape, 0) // rows) % 2
-    lhs = jnp.concatenate(
-        [jnp.where(upper == 0, doubled, 0.0), jnp.where(upper == 1, doubled, 0.0)], axis=1
-    ).astype(BF)
+        latents = got_wide[pl.ds(t, count, stride=tiles), :].astype(BF)
+        values += dot(latents, wv_ref[0, 128 * t : 128 * (t + 1), :])
+    values_wide[...] = values
+    upper[...] = jnp.zeros_like(upper)
+    lower[...] = jnp.zeros_like(lower)
+    for b in range(rows):
+        line = values_wide[pl.ds(b, n_exp, stride=rows), :]
+        upper[pl.ds(b, n_exp, stride=8), :] = line
+        lower[pl.ds(rows + b, n_exp, stride=8), :] = line
+    lhs = jnp.concatenate([upper[...], lower[...]], axis=1).astype(BF)
     half = wo_ref.shape[1] // 2
     step = 512
     for at in range(0, half, step):
@@ -194,17 +188,15 @@
     combine_ref[...] = jnp.concatenate([hi, low], axis=1)
 
 
-def gate_up(got_ref, gain_ref, wg_ref, wu_ref, out_ref):
+def gate_up(got_ref, gain_ref, wg_ref, wu_ref, out_ref, scratch):
     n, span, _ = got_ref.shape
     slots = n * span // 8
     tiles = wg_ref.shape[1] // 128
-    i, j = iota((tiles * slots, n * span), 0), iota((tiles * slots, n * span), 1)
-    pick = ((j // 8 == i % slots) & (j % 8 == i // slots)).astype(BF)
-    rows = dot(pick, got_ref[...].reshape(n * span, 128))
+    scratch[...] = got_ref[...].astype(F32).reshape(n * span, 128)
     sumsq = jnp.zeros((slots, 128), F32)
     scaled = []
     for k in range(tiles):
-        part = rows[slots * k : slots * (k + 1)]
+        part = scratch[pl.ds(k, slots, stride=8), :]
         sumsq += part * part
         scaled.append((part * gain_ref[:, 128 * k : 128 * (k + 1)]).astype(BF))
     scaled = jnp.concatenate(scaled, axis=1)
@@ -234,17 +226,16 @@
         out_ref[c] = active
 
 
-def down(got_ref, wd_ref, out_ref):
+def down(got_ref, wd_ref, out_ref, scratch):
     n_ctx, per, units = got_ref.shape
     slots = n_ctx * per
     tiles = wd_ref.shape[2] // 128
     active = got_ref[...].reshape(slots, units)
-    produced = dot(active, wd_ref[0]).astype(BF)
-    stacked = jnp.concatenate([produced[:, 128 * k : 128 * (k + 1)] for k in range(tiles)], axis=0)
-    size = slots * 8
-    i, j = iota((size, tiles * slots), 0), iota((size, tiles * slots), 1)
-    place = ((i // 8 == j % slots) & (i % 8 == j // slots)).astype(BF)
-    out_ref[...] = dot(place, stacked).astype(BF).reshape(out_ref.shape)
+    produced = dot(active, wd_ref[0])
+    for k in range(tiles):
+        scratch[pl.ds(k, slots, stride=8), :] = produced[:, 128 * k : 128 * (k + 1)]
+    scratch[pl.ds(tiles, slots, stride=8), :] = jnp.zeros((slots, 128), F32)
+    out_ref[...] = scratch[...].astype(BF).reshape(out_ref.shape)
 
 
 def combine_rows(got_ref, combine_ref, hidden_ref, out_ref):
@@ -318,13 +309,25 @@
         compiler_params=pltpu.CompilerParams(vmem_limit_bytes=53 * MIB),
     )(lengths, jnp.swapaxes(queries, 1, 2), jnp.swapaxes(latent_cache, 1, 2))
     got = exchange(sent, "ctx")
-    sent = call(merge, shape_of((n_exp, groups * tiles, 128), BF), (got,), (1 << 22, 1 << 20))
+    sent = call(
+        merge,
+        shape_of((n_exp, groups * tiles, 128), BF),
+        (got,),
+        (1 << 22, 1 << 20),
+        scratch_shapes=[pltpu.VMEM((n_exp * groups * tiles, 128), F32)],
+    )
     got = exchange(sent, "exp")
     sent = call(
         project,
         shape_of((n_exp, 2 * groups, D // 2), BF),
         (got, w_value, w_out),
         (2 * 128 * 256 * D // 2, 2 * 128 * D * 2),
+        scratch_shapes=[
+            pltpu.VMEM((n_exp * groups * tiles, 128), F32),
+            pltpu.VMEM((n_exp * groups, 128), F32),
+            pltpu.VMEM((2 * n_exp * groups, 128), F32),
+            pltpu.VMEM((2 * n_exp * groups, 128), F32),
+        ],
     )
     got = exchange(sent, "exp")
     sent = call(add_heads, shape_of((n_ctx, groups, width), BF), (got,), (1 << 20, 1 << 20))
@@ -343,6 +346,7 @@
         shape_of((n_ctx, slots // n_ctx, 2 * units + 128), BF),
         (got, gain, w_gate, w_up),
         (4 * slots * width * units, 4 * width * units),
+        scratch_shapes=[pltpu.VMEM((slots * 8, 128), F32)],
     )
     got = exchange(sent, "ctx")
     sent = call(activate, shape_of((n_ctx, slots // n_ctx, units), BF), (got,), (1 << 20, 1 << 19))
@@ -352,6 +356,7 @@
         shape_of((experts, 16, 128), BF),
         (got, w_down),
         (2 * slots * width * units, 2 * width * units),
+        scratch_shapes=[pltpu.VMEM((slots * 8, 128), F32)],
     )
     got = exchange(sent, ("row", "exp"))
     return call(

time: 131 us -> 130 us (level)
  no operation moved by 1% of the time
where the time goes in v6:
time: 130 us; the launch traced here: 129 us
  blocking collectives  107 us (82%)
  Pallas kernels  10.8 us (8%)
  starting transfers between devices  5.47 us (4%)
  waiting for transfers between devices  5.31 us (4%)
    all_to_all x7, blocking collectives, exchange(): return lax.all_to_all(x, axes, split_axis=0, concat_axis=0, tiled=True)  107 us
    pallas_call x9, Pallas kernels, call(): pl.pallas_call(kernel, out_shape=out, cost_estimate=pl.CostEstimate(flops...  5.78 us
    all_to_all x1, starting transfers between devices, exchange(): return lax.all_to_all(x, axes, split_axis=0, concat_axis=0, tiled=True)  5.47 us
    all_to_all x1, waiting for transfers between devices, exchange(): return lax.all_to_all(x, axes, split_axis=0, concat_axis=0, tiled=True)  5.31 us
    pallas_call x1, Pallas kernels, on_device(): pl.pallas_call(attend, out_shape=shape_of((n_ctx, span, 128), BF), in_spe...  5.06 us
  transfers between devices with their start and end apart: 1, of which 1 were waited for; matrix products, arithmetic and copies ran while one was open for 0% of the time, Pallas kernels for 1%

profile of v6, /device:TPU:1, one launch (start us, length us, event | category | flops | bytes accessed | tf_op | source)
XLA Modules:
  0.0 129.4 jit_solution(14441237702457554297)
XLA Ops:
  0.0 0.7 copy-done.6
  0.7 5.1 %shard_map.118 = bf16[8,272,128]{2,1,0:T(8,128)(2,1)S(1)} custom-call(s32[4]{0:T(128)S(1)} %copy-done.6, bf16[4,576,128]{2,1,0:T(8,128)(2,1)} %bitcast.3, bf16[4,576,1024]{2,1,0:T(8,128)(2,1)} %bitcast.2), custom_call_target="tpu_custom_call" | custom-call | flops 1140850688 | bytes 5308416 | tf_op jit(solution)/shard_map/pallas_call | solution.py:289
  5.7 0.0 copy-start.2
  5.7 25.4 %all_to_all.40.got_ref = bf16[8,272,128]{2,1,0:T(8,128)(2,1)S(1)} all-to-all(bf16[8,272,128]{2,1,0:T(8,128)(2,1)S(1)} %shard_map.118), channel_id=1, replica_groups=mesh['ctx'=8,'row'=2,'exp'=16] {'ctx'}, dimensions={0} | all-to-all | bytes 1114112 | tf_op jit(solution)/shard_map/all_to_all | solution.py:21
  31.1 0.3 shard_map.119
  31.4 13.1 %all_to_all.41.got_ref = bf16[16,16,128]{2,1,0:T(8,128)(2,1)S(1)} all-to-all(bf16[16,16,128]{2,1,0:T(8,128)(2,1)S(1)} %shard_map.119), channel_id=1, replica_groups=mesh['ctx'=8,'row'=2,'exp'=16] {'exp'}, dimensions={0} | all-to-all | bytes 131072 | tf_op jit(solution)/shard_map/all_to_all | solution.py:21
  44.5 0.6 shard_map.120
  45.1 0.0 copy-start.9
  45.2 0.0 copy-start.8
  45.2 0.0 copy-start
  45.2 13.9 %all_to_all.42.got_ref = bf16[16,8,3584]{2,1,0:T(8,128)(2,1)S(1)} all-to-all(bf16[16,8,3584]{2,1,0:T(8,128)(2,1)S(1)} %shard_map.120), channel_id=1, replica_groups=mesh['ctx'=8,'row'=2,'exp'=16] {'exp'}, dimensions={0} | all-to-all | bytes 1835008 | tf_op jit(solution)/shard_map/all_to_all | solution.py:21
  59.1 0.8 shard_map.121
  59.8 5.5 %all-to-all-start.3 = ((bf16[8,4,896]{2,1,0:T(4,128)(2,1)}), bf16[8,4,896]{2,1,0:T(4,128)(2,1)S(1)}, u32[]{:S(2)}, u32[]{:S(2)}) async-start(bf16[8,4,896]{2,1,0:T(4,128)(2,1)} %shard_map.121), calls=%async_computation.3 | async-start | bytes 114688 | tf_op jit(solution)/shard_map/all_to_all | solution.py:21
  65.3 1.8 %shard_map.122 = (bf16[512,64]{1,0:T(8,128)(2,1)S(1)}, bf16[512,128]{1,0:T(8,128)(2,1)S(1)}) custom-call(s32[4,8]{1,0:T(4,128)S(1)} %copy-done.7, f32[4,8]{1,0:T(4,128)S(1)} %copy-done.8), custom_call_target="tpu_custom_call" | custom-call | flops 3276800 | bytes 204800 | tf_op jit(solution)/shard_map/pallas_call | solution.py:40
  67.1 5.3 %all-to-all-done.3.got_ref = bf16[8,4,896]{2,1,0:T(4,128)(2,1)S(1)} async-done(((bf16[8,4,896]{2,1,0:T(4,128)(2,1)}), bf16[8,4,896]{2,1,0:T(4,128)(2,1)S(1)}, u32[]{:S(2)}, u32[]{:S(2)}) %all-to-all-start.3) | async-done | bytes 57376 | tf_op jit(solution)/shard_map/all_to_all | solution.py:21
  72.5 0.2 shard_map.123
  72.7 16.3 %all_to_all.43.got_ref = bf16[32,16,128]{2,1,0:T(8,128)(2,1)S(1)} all-to-all(bf16[32,16,128]{2,1,0:T(8,128)(2,1)S(1)} %get-tuple-element.10), channel_id=1, replica_groups=mesh['ctx'=8,'row'=2,'exp'=16] {'row','exp'}, dimensions={0} | all-to-all | bytes 262144 | tf_op jit(solution)/shard_map/all_to_all | solution.py:21
  88.9 0.8 shard_map.124
  89.7 14.4 %all_to_all.44.got_ref = bf16[8,8,2176]{2,1,0:T(8,128)(2,1)S(1)} all-to-all(bf16[8,8,2176]{2,1,0:T(8,128)(2,1)S(1)} %shard_map.124), channel_id=1, replica_groups=mesh['ctx'=8,'row'=2,'exp'=16] {'ctx'}, dimensions={0} | all-to-all | bytes 557056 | tf_op jit(solution)/shard_map/all_to_all | solution.py:21
  104.1 0.1 shard_map.125
  104.2 10.3 %all_to_all.45.got_ref = bf16[8,8,1024]{2,1,0:T(8,128)(2,1)S(1)} all-to-all(bf16[8,8,1024]{2,1,0:T(8,128)(2,1)S(1)} %shard_map.125), channel_id=1, replica_groups=mesh['ctx'=8,'row'=2,'exp'=16] {'ctx'}, dimensions={0} | all-to-all | bytes 262144 | tf_op jit(solution)/shard_map/all_to_all | solution.py:21
  114.5 0.4 shard_map.126
  115.0 13.6 %all_to_all.46.got_ref = bf16[32,16,128]{2,1,0:T(8,128)(2,1)S(1)} all-to-all(bf16[32,16,128]{2,1,0:T(8,128)(2,1)S(1)} %shard_map.126), channel_id=1, replica_groups=mesh['ctx'=8,'row'=2,'exp'=16] {'row','exp'}, dimensions={0} | all-to-all | bytes 262144 | tf_op jit(solution)/shard_map/all_to_all | solution.py:21
  128.6 0.8 shard_map.127
  (16 shorter events, 0.0 us)
Async XLA Ops:
  0.0 0.7 copy-start.6
  0.7 43.9 %copy-start.4 = (bf16[1,512,128]{2,1,0:T(8,128)(2,1)S(1)}, bf16[1,512,128]{2,1,0:T(8,128)(2,1)}, u32[]{:S(2)}) copy-start(bf16[1,512,128]{2,1,0:T(8,128)(2,1)} %wv_ref.1) | copy-start | bytes 393220
  5.7 38.8 %copy-start.2 = (bf16[128,7168]{1,0:T(8,128)(2,1)S(1)}, bf16[128,7168]{1,0:T(8,128)(2,1)}, u32[]{:S(2)}) copy-start(bf16[128,7168]{1,0:T(8,128)(2,1)} %wo_ref.1) | copy-start | bytes 5505028
  45.1 20.2 %copy-start.9 = (f32[896]{0:T(1024)S(1)}, f32[896]{0:T(1024)}, u32[]{:S(2)}) copy-start(f32[896]{0:T(1024)} %param.18) | copy-start | bytes 10756
  45.2 20.2 %copy-start.7 = (s32[4,8]{1,0:T(4,128)S(1)}, s32[4,8]{1,0:T(4,128)}, u32[]{:S(2)}) copy-start(s32[4,8]{1,0:T(4,128)} %ids_ref.1) | copy-start | bytes 388
  45.2 20.2 %copy-start.8 = (f32[4,8]{1,0:T(4,128)S(1)}, f32[4,8]{1,0:T(4,128)}, u32[]{:S(2)}) copy-start(f32[4,8]{1,0:T(4,128)} %weights_ref.1) | copy-start | bytes 388
  45.2 27.3 %copy-start = (bf16[1,896,1024]{2,1,0:T(8,128)(2,1)S(1)}, bf16[1,896,1024]{2,1,0:T(8,128)(2,1)}, u32[]{:S(2)}) copy-start(bf16[1,896,1024]{2,1,0:T(8,128)(2,1)} %wu_ref.1) | copy-start | bytes 5505028
  45.2 27.3 %copy-start.5 = (bf16[4,896]{1,0:T(4,128)(2,1)S(1)}, bf16[4,896]{1,0:T(4,128)(2,1)}, u32[]{:S(2)}) copy-start(bf16[4,896]{1,0:T(4,128)(2,1)} %stream_ref.1) | copy-start | bytes 21508
  59.8 12.6 %all-to-all-start.3 = ((bf16[8,4,896]{2,1,0:T(4,128)(2,1)}), bf16[8,4,896]{2,1,0:T(4,128)(2,1)S(1)}, u32[]{:S(2)}, u32[]{:S(2)}) async-start(bf16[8,4,896]{2,1,0:T(4,128)(2,1)} %shard_map.121), calls=%async_computation.3 | async-start | bytes 114688 | tf_op jit(solution)/shard_map/all_to_all | solution.py:21
  72.4 16.5 %copy-start.1 = (bf16[1,896,1024]{2,1,0:T(8,128)(2,1)S(1)}, bf16[1,896,1024]{2,1,0:T(8,128)(2,1)}, u32[]{:S(2)}) copy-start(bf16[1,896,1024]{2,1,0:T(8,128)(2,1)} %wg_ref.1) | copy-start | bytes 5505028
  88.9 25.6 %copy-start.3 = (bf16[1,1024,896]{2,1,0:T(8,128)(2,1)S(1)}, bf16[1,1024,896]{2,1,0:T(8,128)(2,1)}, u32[]{:S(2)}) copy-start(bf16[1,1024,896]{2,1,0:T(8,128)(2,1)} %wd_ref.1) | copy-start | bytes 5505028

commit v7 on v6

--- a/solution.py
+++ b/solution.py
@@ -72,10 +72,17 @@
     first = lax.axis_index("ctx") * block
     lane = iota((heads, 128), 1)
     stat = jnp.zeros((heads, 128), F32)
-    for r in range(rows):
+
+    def products(r):
         for copy in copies[r]:
             copy.wait()
-        scores = dot(q_ref[r], kv_ref[r], ((0,), (0,))) * QK_HEAD ** (-0.5)
+        return dot(q_ref[r], kv_ref[r], ((0,), (0,))) * QK_HEAD ** (-0.5)
+
+    following = products(0)
+    for r in range(rows):
+        scores = following
+        if r + 1 < rows:
+            following = products(r + 1)
         live = iota((heads, block), 1) < length_ref[r] - first
         scores = jnp.where(live, scores, DEAD)
         top = jnp.max(scores, axis=1, keepdims=True)

time: 130 us -> 129 us (level)
  no operation moved by 1% of the time
where the time goes in v7:
time: 129 us
  blocking collectives  107 us (83%)
  Pallas kernels  10.4 us (8%)
  starting transfers between devices  5.46 us (4%)
  waiting for transfers between devices  5.31 us (4%)
    all_to_all x7, blocking collectives, exchange(): return lax.all_to_all(x, axes, split_axis=0, concat_axis=0, tiled=True)  107 us
    pallas_call x9, Pallas kernels, call(): pl.pallas_call(kernel, out_shape=out, cost_estimate=pl.CostEstimate(flops...  5.78 us
    all_to_all x1, starting transfers between devices, exchange(): return lax.all_to_all(x, axes, split_axis=0, concat_axis=0, tiled=True)  5.46 us
    all_to_all x1, waiting for transfers between devices, exchange(): return lax.all_to_all(x, axes, split_axis=0, concat_axis=0, tiled=True)  5.31 us
    pallas_call x1, Pallas kernels, on_device(): pl.pallas_call(attend, out_shape=shape_of((n_ctx, span, 128), BF), in_spe...  4.65 us
  transfers between devices with their start and end apart: 1, of which 1 were waited for; matrix products, arithmetic and copies ran while one was open for 0% of the time, Pallas kernels for 1%

profile of v7, /device:TPU:1, one launch (start us, length us, event | category | flops | bytes accessed | tf_op | source)
XLA Modules:
  0.0 129.0 jit_solution(1303334263028186197)
XLA Ops:
  0.0 0.7 copy-done.6
  0.7 4.7 %shard_map.118 = bf16[8,272,128]{2,1,0:T(8,128)(2,1)S(1)} custom-call(s32[4]{0:T(128)S(1)} %copy-done.6, bf16[4,576,128]{2,1,0:T(8,128)(2,1)} %bitcast.3, bf16[4,576,1024]{2,1,0:T(8,128)(2,1)} %bitcast.2), custom_call_target="tpu_custom_call" | custom-call | flops 1140850688 | bytes 5308416 | tf_op jit(solution)/shard_map/pallas_call | solution.py:296
  5.3 0.0 copy-start.2
  5.3 25.4 %all_to_all.40.got_ref = bf16[8,272,128]{2,1,0:T(8,128)(2,1)S(1)} all-to-all(bf16[8,272,128]{2,1,0:T(8,128)(2,1)S(1)} %shard_map.118), channel_id=1, replica_groups=mesh['ctx'=8,'row'=2,'exp'=16] {'ctx'}, dimensions={0} | all-to-all | bytes 1114112 | tf_op jit(solution)/shard_map/all_to_all | solution.py:21
  30.8 0.3 shard_map.119
  31.0 13.1 %all_to_all.41.got_ref = bf16[16,16,128]{2,1,0:T(8,128)(2,1)S(1)} all-to-all(bf16[16,16,128]{2,1,0:T(8,128)(2,1)S(1)} %shard_map.119), channel_id=1, replica_groups=mesh['ctx'=8,'row'=2,'exp'=16] {'exp'}, dimensions={0} | all-to-all | bytes 131072 | tf_op jit(solution)/shard_map/all_to_all | solution.py:21
  44.1 0.6 shard_map.120
  44.7 0.0 copy-start.9
  44.7 0.0 copy-start.7
  44.8 0.0 copy-start.8
  44.8 13.9 %all_to_all.42.got_ref = bf16[16,8,3584]{2,1,0:T(8,128)(2,1)S(1)} all-to-all(bf16[16,8,3584]{2,1,0:T(8,128)(2,1)S(1)} %shard_map.120), channel_id=1, replica_groups=mesh['ctx'=8,'row'=2,'exp'=16] {'exp'}, dimensions={0} | all-to-all | bytes 1835008 | tf_op jit(solution)/shard_map/all_to_all | solution.py:21
  58.7 0.8 shard_map.121
  59.4 5.5 %all-to-all-start.3 = ((bf16[8,4,896]{2,1,0:T(4,128)(2,1)}), bf16[8,4,896]{2,1,0:T(4,128)(2,1)S(1)}, u32[]{:S(2)}, u32[]{:S(2)}) async-start(bf16[8,4,896]{2,1,0:T(4,128)(2,1)} %shard_map.121), calls=%async_computation.3 | async-start | bytes 114688 | tf_op jit(solution)/shard_map/all_to_all | solution.py:21
  64.9 1.8 %shard_map.122 = (bf16[512,64]{1,0:T(8,128)(2,1)S(1)}, bf16[512,128]{1,0:T(8,128)(2,1)S(1)}) custom-call(s32[4,8]{1,0:T(4,128)S(1)} %copy-done.7, f32[4,8]{1,0:T(4,128)S(1)} %copy-done.8), custom_call_target="tpu_custom_call" | custom-call | flops 3276800 | bytes 204800 | tf_op jit(solution)/shard_map/pallas_call | solution.py:40
  66.7 5.3 %all-to-all-done.3.got_ref = bf16[8,4,896]{2,1,0:T(4,128)(2,1)S(1)} async-done(((bf16[8,4,896]{2,1,0:T(4,128)(2,1)}), bf16[8,4,896]{2,1,0:T(4,128)(2,1)S(1)}, u32[]{:S(2)}, u32[]{:S(2)}) %all-to-all-start.3) | async-done | bytes 57376 | tf_op jit(solution)/shard_map/all_to_all | solution.py:21
  72.0 0.2 shard_map.123
  72.2 16.3 %all_to_all.43.got_ref = bf16[32,16,128]{2,1,0:T(8,128)(2,1)S(1)} all-to-all(bf16[32,16,128]{2,1,0:T(8,128)(2,1)S(1)} %get-tuple-element.10), channel_id=1, replica_groups=mesh['ctx'=8,'row'=2,'exp'=16] {'row','exp'}, dimensions={0} | all-to-all | bytes 262144 | tf_op jit(solution)/shard_map/all_to_all | solution.py:21
  88.5 0.8 shard_map.124
  89.3 14.4 %all_to_all.44.got_ref = bf16[8,8,2176]{2,1,0:T(8,128)(2,1)S(1)} all-to-all(bf16[8,8,2176]{2,1,0:T(8,128)(2,1)S(1)} %shard_map.124), channel_id=1, replica_groups=mesh['ctx'=8,'row'=2,'exp'=16] {'ctx'}, dimensions={0} | all-to-all | bytes 557056 | tf_op jit(solution)/shard_map/all_to_all | solution.py:21
  103.6 0.1 shard_map.125
  103.8 10.3 %all_to_all.45.got_ref = bf16[8,8,1024]{2,1,0:T(8,128)(2,1)S(1)} all-to-all(bf16[8,8,1024]{2,1,0:T(8,128)(2,1)S(1)} %shard_map.125), channel_id=1, replica_groups=mesh['ctx'=8,'row'=2,'exp'=16] {'ctx'}, dimensions={0} | all-to-all | bytes 262144 | tf_op jit(solution)/shard_map/all_to_all | solution.py:21
  114.1 0.4 shard_map.126
  114.6 13.6 %all_to_all.46.got_ref = bf16[32,16,128]{2,1,0:T(8,128)(2,1)S(1)} all-to-all(bf16[32,16,128]{2,1,0:T(8,128)(2,1)S(1)} %shard_map.126), channel_id=1, replica_groups=mesh['ctx'=8,'row'=2,'exp'=16] {'row','exp'}, dimensions={0} | all-to-all | bytes 262144 | tf_op jit(solution)/shard_map/all_to_all | solution.py:21
  128.2 0.8 shard_map.127
  (16 shorter events, 0.0 us)
Async XLA Ops:
  0.0 0.7 copy-start.6
  0.7 43.4 %copy-start.4 = (bf16[1,512,128]{2,1,0:T(8,128)(2,1)S(1)}, bf16[1,512,128]{2,1,0:T(8,128)(2,1)}, u32[]{:S(2)}) copy-start(bf16[1,512,128]{2,1,0:T(8,128)(2,1)} %wv_ref.1) | copy-start | bytes 393220
  5.3 38.8 %copy-start.2 = (bf16[128,7168]{1,0:T(8,128)(2,1)S(1)}, bf16[128,7168]{1,0:T(8,128)(2,1)}, u32[]{:S(2)}) copy-start(bf16[128,7168]{1,0:T(8,128)(2,1)} %wo_ref.1) | copy-start | bytes 5505028
  44.7 20.2 %copy-start.9 = (f32[896]{0:T(1024)S(1)}, f32[896]{0:T(1024)}, u32[]{:S(2)}) copy-start(f32[896]{0:T(1024)} %param.18) | copy-start | bytes 10756
  44.7 20.2 %copy-start.7 = (s32[4,8]{1,0:T(4,128)S(1)}, s32[4,8]{1,0:T(4,128)}, u32[]{:S(2)}) copy-start(s32[4,8]{1,0:T(4,128)} %ids_ref.1) | copy-start | bytes 388
  44.8 20.2 %copy-start.8 = (f32[4,8]{1,0:T(4,128)S(1)}, f32[4,8]{1,0:T(4,128)}, u32[]{:S(2)}) copy-start(f32[4,8]{1,0:T(4,128)} %weights_ref.1) | copy-start | bytes 388
  44.8 27.3 %copy-start = (bf16[1,896,1024]{2,1,0:T(8,128)(2,1)S(1)}, bf16[1,896,1024]{2,1,0:T(8,128)(2,1)}, u32[]{:S(2)}) copy-start(bf16[1,896,1024]{2,1,0:T(8,128)(2,1)} %wu_ref.1) | copy-start | bytes 5505028
  44.8 27.3 %copy-start.5 = (bf16[4,896]{1,0:T(4,128)(2,1)S(1)}, bf16[4,896]{1,0:T(4,128)(2,1)}, u32[]{:S(2)}) copy-start(bf16[4,896]{1,0:T(4,128)(2,1)} %stream_ref.1) | copy-start | bytes 21508
  59.4 12.6 %all-to-all-start.3 = ((bf16[8,4,896]{2,1,0:T(4,128)(2,1)}), bf16[8,4,896]{2,1,0:T(4,128)(2,1)S(1)}, u32[]{:S(2)}, u32[]{:S(2)}) async-start(bf16[8,4,896]{2,1,0:T(4,128)(2,1)} %shard_map.121), calls=%async_computation.3 | async-start | bytes 114688 | tf_op jit(solution)/shard_map/all_to_all | solution.py:21
  72.0 16.5 %copy-start.1 = (bf16[1,896,1024]{2,1,0:T(8,128)(2,1)S(1)}, bf16[1,896,1024]{2,1,0:T(8,128)(2,1)}, u32[]{:S(2)}) copy-start(bf16[1,896,1024]{2,1,0:T(8,128)(2,1)} %wg_ref.1) | copy-start | bytes 5505028
  88.5 25.6 %copy-start.3 = (bf16[1,1024,896]{2,1,0:T(8,128)(2,1)S(1)}, bf16[1,1024,896]{2,1,0:T(8,128)(2,1)}, u32[]{:S(2)}) copy-start(bf16[1,1024,896]{2,1,0:T(8,128)(2,1)} %wd_ref.1) | copy-start | bytes 5505028

commit v8 on v7

--- a/solution.py
+++ b/solution.py
@@ -14,6 +14,7 @@
 I32 = jnp.int32
 epsilon = 1e-06
 DEAD = -1e30
+LOG2E = 1.4426950408889634
 MIB = 1024 * 1024
 
 
@@ -76,8 +77,9 @@
     def products(r):
         for copy in copies[r]:
             copy.wait()
-        return dot(q_ref[r], kv_ref[r], ((0,), (0,))) * QK_HEAD ** (-0.5)
-
+        return dot(q_ref[r], kv_ref[r], ((0,), (0,)))
+
+    scale = QK_HEAD ** (-0.5)
     following = products(0)
     for r in range(rows):
         scores = following
@@ -86,12 +88,12 @@
         live = iota((heads, block), 1) < length_ref[r] - first
         scores = jnp.where(live, scores, DEAD)
         top = jnp.max(scores, axis=1, keepdims=True)
-        weights = jnp.where(live, jnp.exp(scores - top), 0.0)
+        weights = jnp.exp2((scores - jnp.maximum(top, 0.5 * DEAD)) * (scale * LOG2E))
         total = jnp.sum(weights, axis=1, keepdims=True)
         safe = jnp.where(total > 0, total, 1.0)
         part = dot(weights.astype(BF), kv_ref[r, :latent, :], ((1,), (1,))) * (1.0 / safe)
         part = part.astype(BF)
-        for p, piece in enumerate(pieces(top + jnp.log(safe))):
+        for p, piece in enumerate(pieces(top * scale + jnp.log(safe))):
             stat = jnp.where(lane == 4 * r + p, piece, stat)
         for c in range(n_ctx):
             for t in range(tiles):

time: 129 us -> 129 us (level)
  no operation moved by 1% of the time
where the time goes in v8:
time: 129 us
  blocking collectives  107 us (83%)
  Pallas kernels  10.3 us (8%)
  starting transfers between devices  5.46 us (4%)
  waiting for transfers between devices  5.31 us (4%)
    all_to_all x7, blocking collectives, exchange(): return lax.all_to_all(x, axes, split_axis=0, concat_axis=0, tiled=True)  107 us
    pallas_call x9, Pallas kernels, call(): pl.pallas_call(kernel, out_shape=out, cost_estimate=pl.CostEstimate(flops...  5.78 us
    all_to_all x1, starting transfers between devices, exchange(): return lax.all_to_all(x, axes, split_axis=0, concat_axis=0, tiled=True)  5.46 us
    all_to_all x1, waiting for transfers between devices, exchange(): return lax.all_to_all(x, axes, split_axis=0, concat_axis=0, tiled=True)  5.31 us
    pallas_call x1, Pallas kernels, on_device(): pl.pallas_call(attend, out_shape=shape_of((n_ctx, span, 128), BF), in_spe...  4.49 us
  transfers between devices with their start and end apart: 1, of which 1 were waited for; matrix products, arithmetic and copies ran while one was open for 0% of the time, Pallas kernels for 1%

profile of v8, /device:TPU:1, one launch (start us, length us, event | category | flops | bytes accessed | tf_op | source)
XLA Modules:
  0.0 128.8 jit_solution(17504389776536322731)
XLA Ops:
  0.0 0.7 copy-done.6
  0.7 4.5 %shard_map.118 = bf16[8,272,128]{2,1,0:T(8,128)(2,1)S(1)} custom-call(s32[4]{0:T(128)S(1)} %copy-done.6, bf16[4,576,128]{2,1,0:T(8,128)(2,1)} %bitcast.3, bf16[4,576,1024]{2,1,0:T(8,128)(2,1)} %bitcast.2), custom_call_target="tpu_custom_call" | custom-call | flops 1140850688 | bytes 5308416 | tf_op jit(solution)/shard_map/pallas_call | solution.py:298
  5.2 0.0 copy-start.2
  5.2 25.4 %all_to_all.40.got_ref = bf16[8,272,128]{2,1,0:T(8,128)(2,1)S(1)} all-to-all(bf16[8,272,128]{2,1,0:T(8,128)(2,1)S(1)} %shard_map.118), channel_id=1, replica_groups=mesh['ctx'=8,'row'=2,'exp'=16] {'ctx'}, dimensions={0} | all-to-all | bytes 1114112 | tf_op jit(solution)/shard_map/all_to_all | solution.py:22
  30.6 0.3 shard_map.119
  30.8 13.1 %all_to_all.41.got_ref = bf16[16,16,128]{2,1,0:T(8,128)(2,1)S(1)} all-to-all(bf16[16,16,128]{2,1,0:T(8,128)(2,1)S(1)} %shard_map.119), channel_id=1, replica_groups=mesh['ctx'=8,'row'=2,'exp'=16] {'exp'}, dimensions={0} | all-to-all | bytes 131072 | tf_op jit(solution)/shard_map/all_to_all | solution.py:22
  44.0 0.6 shard_map.120
  44.6 0.0 copy-start.9
  44.6 0.0 copy-start.8
  44.6 0.0 copy-start
  44.6 13.9 %all_to_all.42.got_ref = bf16[16,8,3584]{2,1,0:T(8,128)(2,1)S(1)} all-to-all(bf16[16,8,3584]{2,1,0:T(8,128)(2,1)S(1)} %shard_map.120), channel_id=1, replica_groups=mesh['ctx'=8,'row'=2,'exp'=16] {'exp'}, dimensions={0} | all-to-all | bytes 1835008 | tf_op jit(solution)/shard_map/all_to_all | solution.py:22
  58.5 0.8 shard_map.121
  59.3 5.5 %all-to-all-start.3 = ((bf16[8,4,896]{2,1,0:T(4,128)(2,1)}), bf16[8,4,896]{2,1,0:T(4,128)(2,1)S(1)}, u32[]{:S(2)}, u32[]{:S(2)}) async-start(bf16[8,4,896]{2,1,0:T(4,128)(2,1)} %shard_map.121), calls=%async_computation.3 | async-start | bytes 114688 | tf_op jit(solution)/shard_map/all_to_all | solution.py:22
  64.8 1.8 %shard_map.122 = (bf16[512,64]{1,0:T(8,128)(2,1)S(1)}, bf16[512,128]{1,0:T(8,128)(2,1)S(1)}) custom-call(s32[4,8]{1,0:T(4,128)S(1)} %copy-done.7, f32[4,8]{1,0:T(4,128)S(1)} %copy-done.8), custom_call_target="tpu_custom_call" | custom-call | flops 3276800 | bytes 204800 | tf_op jit(solution)/shard_map/pallas_call | solution.py:41
  66.6 5.3 %all-to-all-done.3.got_ref = bf16[8,4,896]{2,1,0:T(4,128)(2,1)S(1)} async-done(((bf16[8,4,896]{2,1,0:T(4,128)(2,1)}), bf16[8,4,896]{2,1,0:T(4,128)(2,1)S(1)}, u32[]{:S(2)}, u32[]{:S(2)}) %all-to-all-start.3) | async-done | bytes 57376 | tf_op jit(solution)/shard_map/all_to_all | solution.py:22
  71.9 0.2 shard_map.123
  72.1 16.2 %all_to_all.43.got_ref = bf16[32,16,128]{2,1,0:T(8,128)(2,1)S(1)} all-to-all(bf16[32,16,128]{2,1,0:T(8,128)(2,1)S(1)} %get-tuple-element.10), channel_id=1, replica_groups=mesh['ctx'=8,'row'=2,'exp'=16] {'row','exp'}, dimensions={0} | all-to-all | bytes 262144 | tf_op jit(solution)/shard_map/all_to_all | solution.py:22
  88.3 0.8 shard_map.124
  89.1 14.4 %all_to_all.44.got_ref = bf16[8,8,2176]{2,1,0:T(8,128)(2,1)S(1)} all-to-all(bf16[8,8,2176]{2,1,0:T(8,128)(2,1)S(1)} %shard_map.124), channel_id=1, replica_groups=mesh['ctx'=8,'row'=2,'exp'=16] {'ctx'}, dimensions={0} | all-to-all | bytes 557056 | tf_op jit(solution)/shard_map/all_to_all | solution.py:22
  103.5 0.1 shard_map.125
  103.6 10.3 %all_to_all.45.got_ref = bf16[8,8,1024]{2,1,0:T(8,128)(2,1)S(1)} all-to-all(bf16[8,8,1024]{2,1,0:T(8,128)(2,1)S(1)} %shard_map.125), channel_id=1, replica_groups=mesh['ctx'=8,'row'=2,'exp'=16] {'ctx'}, dimensions={0} | all-to-all | bytes 262144 | tf_op jit(solution)/shard_map/all_to_all | solution.py:22
  114.0 0.4 shard_map.126
  114.4 13.6 %all_to_all.46.got_ref = bf16[32,16,128]{2,1,0:T(8,128)(2,1)S(1)} all-to-all(bf16[32,16,128]{2,1,0:T(8,128)(2,1)S(1)} %shard_map.126), channel_id=1, replica_groups=mesh['ctx'=8,'row'=2,'exp'=16] {'row','exp'}, dimensions={0} | all-to-all | bytes 262144 | tf_op jit(solution)/shard_map/all_to_all | solution.py:22
  128.0 0.8 shard_map.127
  (16 shorter events, 0.0 us)
Async XLA Ops:
  0.0 0.7 copy-start.6
  0.7 43.3 %copy-start.4 = (bf16[1,512,128]{2,1,0:T(8,128)(2,1)S(1)}, bf16[1,512,128]{2,1,0:T(8,128)(2,1)}, u32[]{:S(2)}) copy-start(bf16[1,512,128]{2,1,0:T(8,128)(2,1)} %wv_ref.1) | copy-start | bytes 393220
  5.2 38.8 %copy-start.2 = (bf16[128,7168]{1,0:T(8,128)(2,1)S(1)}, bf16[128,7168]{1,0:T(8,128)(2,1)}, u32[]{:S(2)}) copy-start(bf16[128,7168]{1,0:T(8,128)(2,1)} %wo_ref.1) | copy-start | bytes 5505028
  44.6 20.2 %copy-start.9 = (f32[896]{0:T(1024)S(1)}, f32[896]{0:T(1024)}, u32[]{:S(2)}) copy-start(f32[896]{0:T(1024)} %param.18) | copy-start | bytes 10756
  44.6 20.2 %copy-start.7 = (s32[4,8]{1,0:T(4,128)S(1)}, s32[4,8]{1,0:T(4,128)}, u32[]{:S(2)}) copy-start(s32[4,8]{1,0:T(4,128)} %ids_ref.1) | copy-start | bytes 388
  44.6 20.2 %copy-start.8 = (f32[4,8]{1,0:T(4,128)S(1)}, f32[4,8]{1,0:T(4,128)}, u32[]{:S(2)}) copy-start(f32[4,8]{1,0:T(4,128)} %weights_ref.1) | copy-start | bytes 388
  44.6 27.3 %copy-start = (bf16[1,896,1024]{2,1,0:T(8,128)(2,1)S(1)}, bf16[1,896,1024]{2,1,0:T(8,128)(2,1)}, u32[]{:S(2)}) copy-start(bf16[1,896,1024]{2,1,0:T(8,128)(2,1)} %wu_ref.1) | copy-start | bytes 5505028
  44.6 27.3 %copy-start.5 = (bf16[4,896]{1,0:T(4,128)(2,1)S(1)}, bf16[4,896]{1,0:T(4,128)(2,1)}, u32[]{:S(2)}) copy-start(bf16[4,896]{1,0:T(4,128)(2,1)} %stream_ref.1) | copy-start | bytes 21508
  59.3 12.6 %all-to-all-start.3 = ((bf16[8,4,896]{2,1,0:T(4,128)(2,1)}), bf16[8,4,896]{2,1,0:T(4,128)(2,1)S(1)}, u32[]{:S(2)}, u32[]{:S(2)}) async-start(bf16[8,4,896]{2,1,0:T(4,128)(2,1)} %shard_map.121), calls=%async_computation.3 | async-start | bytes 114688 | tf_op jit(solution)/shard_map/all_to_all | solution.py:22
  71.9 16.5 %copy-start.1 = (bf16[1,896,1024]{2,1,0:T(8,128)(2,1)S(1)}, bf16[1,896,1024]{2,1,0:T(8,128)(2,1)}, u32[]{:S(2)}) copy-start(bf16[1,896,1024]{2,1,0:T(8,128)(2,1)} %wg_ref.1) | copy-start | bytes 5505028
  88.3 25.6 %copy-start.3 = (bf16[1,1024,896]{2,1,0:T(8,128)(2,1)S(1)}, bf16[1,1024,896]{2,1,0:T(8,128)(2,1)}, u32[]{:S(2)}) copy-start(bf16[1,1024,896]{2,1,0:T(8,128)(2,1)} %wd_ref.1) | copy-start | bytes 5505028
